TPU v7x, 32 devices: a whole 2x2x4 slice. The times are simulated.
32 devices in a mesh: bx: 8 (over y, x, core), by: 4 (over z).
Axes of the slice: x: 2, y: 2, z: 4, core: 2. Of those that a mesh axis runs over, the one named last changes fastest.
Arguments:
- particle_values: float32 [3, 65536], P(None, ('bx', 'by')), may hold values from -6 to 6
- destination: int32 [65536, 1], P(('bx', 'by')), may hold values from 0 to 31; in each aligned block of 2048 rows (0 to 2047, 2048 to 4095, ...) at most 128 rows name the same one
- cell_index: int32 [65536], P(('bx', 'by')), may hold values from 0 to 16383
- weight_in: bfloat16 [3, 3, 64, 9], replicated, may hold values from -0.625 to 0.625
- weight_mid: bfloat16 [3, 3, 64, 192], replicated, may hold values from -0.15625 to 0.15625
- weight_out: bfloat16 [3, 3, 64, 192], replicated, may hold values from -0.15625 to 0.15625
Outputs:
- spectrum: bfloat16 [2, 64, 16, 64, 512], P(None, None, 'bx', None, 'by')
Inputs may be any that keep to these rules, and one draw needn't show every extreme that they name: `destination`: among the 2048 rows of one device, no brick is named more than 128 times; some brick is named exactly 128 times.
All inputs are finite; a program needn't handle non-finite values.
Results may differ from a plain program's by a relative error of at most 0.0074.
Values may be sent and summed in bfloat16 or wider, within the bound.
A program may use at most 192 MiB of HBM per device.

v0:
```python
import math

import jax
import jax.numpy as jnp
from jax import lax
from jax.sharding import PartitionSpec as P

CELL_X = 8
CELL_Y = 128
CELL_Z = 16


def extended(cells, sides, width):
    for axis, dim in sides:
        count = lax.axis_size(axis)
        head = lax.slice_in_dim(cells, 0, width, axis=dim)
        tail = lax.slice_in_dim(cells, cells.shape[dim] - width, cells.shape[dim], axis=dim)
        cells = jnp.concatenate(
            [
                lax.ppermute(tail, axis, [(i, (i + 1) % count) for i in range(count)]),
                cells,
                lax.ppermute(head, axis, [((i + 1) % count, i) for i in range(count)]),
            ],
            axis=dim,
        )
    return cells


def convolve(widened, weight, spacing):
    out_x = widened.shape[2] - 2 * spacing
    out_y = widened.shape[3] - 2 * spacing
    stacked = jnp.concatenate(
        [jnp.roll(widened, spacing, axis=1), widened, jnp.roll(widened, -spacing, axis=1)], axis=0
    )
    summed = None
    for step_x in range(3):
        for step_y in range(3):
            window = lax.slice_in_dim(stacked, step_x * spacing, step_x * spacing + out_x, axis=2)
            window = lax.slice_in_dim(window, step_y * spacing, step_y * spacing + out_y, axis=3)
            product_term = jnp.einsum(
                "oc,czxy->ozxy", weight[step_x, step_y], window, preferred_element_type=jnp.float32
            )
            summed = product_term if summed is None else summed + product_term
    return jnp.where(summed > 0, summed, 0.1 * summed).astype(jnp.bfloat16)


def twiddle_table(count):
    position = jnp.arange(count, dtype=jnp.int32)
    phase = position[:, None] * position[None, :] % count
    angle = phase.astype(jnp.float32) * (2.0 * math.pi / count)
    factor = 1.0 / math.sqrt(count)
    return jnp.stack([jnp.cos(angle) * factor, -jnp.sin(angle) * factor]).astype(jnp.bfloat16)


def transform(moved_rows):
    twiddle = twiddle_table(moved_rows.shape[2])
    return jnp.einsum(
        "tkx,czxy->tczky", twiddle, moved_rows, preferred_element_type=jnp.float32
    ).astype(jnp.bfloat16)


def pack_rows(packed, target_dev, devices_all, capacity):
    width_rows = packed.shape[0]
    rows_here = packed.shape[1]
    block_rows = min(rows_here, 1024)
    block_count = rows_here // block_rows
    bricks = jnp.arange(devices_all, dtype=jnp.int32)
    brick_hot = (
        (target_dev[:, None] == bricks[None, :])
        .astype(jnp.bfloat16)
        .reshape(block_count, block_rows, devices_all)
    )
    block_total = jnp.sum(brick_hot.astype(jnp.float32), axis=1)
    block_start = jnp.cumsum(block_total, axis=0) - block_total
    row_ids = jnp.arange(block_rows, dtype=jnp.int32)
    lower_tri = (row_ids[:, None] > row_ids[None, :]).astype(jnp.bfloat16)
    slot_ids = jnp.arange(capacity, dtype=jnp.int32)
    packed_blocks = jnp.transpose(packed.reshape(width_rows, block_count, block_rows), (1, 0, 2))

    def pack_one_block(carry, pieces):
        hot_block, start_block, data_block = pieces
        prefix = jnp.dot(lower_tri, hot_block, preferred_element_type=jnp.float32)
        hot_float = hot_block.astype(jnp.float32)
        slot_float = jnp.sum(hot_float * (prefix + start_block[None, :]), axis=1)
        slot_hot = (slot_float.astype(jnp.int32)[:, None] == slot_ids[None, :]).astype(jnp.float32)
        spread = jnp.einsum("wp,ps->pws", data_block, slot_hot).reshape(
            block_rows, width_rows * capacity
        )
        added = jnp.dot(
            hot_float.T, spread, precision=lax.Precision.HIGHEST, preferred_element_type=jnp.float32
        )
        return (carry + added, None)

    initial = jnp.zeros((devices_all, width_rows * capacity), jnp.float32)
    outgoing, _ = lax.scan(pack_one_block, initial, (brick_hot, block_start, packed_blocks))
    return outgoing.reshape(devices_all, width_rows, capacity)


def paint_rows(incoming):
    width_rows = incoming.shape[1]
    comps = width_rows - 1
    rows_all = jnp.transpose(incoming, (0, 2, 1)).reshape(-1, width_rows)
    total_rows = rows_all.shape[0]
    block_rows = min(total_rows, 2048)
    block_count = total_rows // block_rows
    high_count = CELL_Z * CELL_X
    high_ids = jnp.arange(high_count, dtype=jnp.int32)
    low_ids = jnp.arange(CELL_Y, dtype=jnp.int32)
    row_blocks = rows_all.reshape(block_count, block_rows, width_rows)

    def paint_one_block(carry, block):
        cells = block[:, 0].astype(jnp.int32)
        values = block[:, 1:]
        high_hot = ((cells // CELL_Y)[:, None] == high_ids[None, :]).astype(jnp.float32)
        low_hot = ((cells % CELL_Y)[:, None] == low_ids[None, :]).astype(jnp.float32)
        spread = jnp.einsum("pf,py->pfy", values, low_hot).reshape(block_rows, comps * CELL_Y)
        added = jnp.dot(
            high_hot.T, spread, precision=lax.Precision.HIGHEST, preferred_element_type=jnp.float32
        )
        return (carry + added, None)

    initial = jnp.zeros((high_count, comps * CELL_Y), jnp.float32)
    summed, _ = lax.scan(paint_one_block, initial, row_blocks)
    painted = jnp.transpose(summed.reshape(high_count, comps, CELL_Y), (1, 0, 2))
    return painted.reshape(comps, CELL_Z, CELL_X, CELL_Y).astype(jnp.bfloat16)


def on_device(particle_values, destination, cell_index, weight_in, weight_mid, weight_out):
    count_x = lax.axis_size("bx")
    count_y = lax.axis_size("by")
    devices_all = count_x * count_y
    rows_here = cell_index.shape[0]
    capacity = 2 * rows_here // devices_all
    target_dev = destination[:, 0]
    packed = jnp.concatenate([cell_index.astype(jnp.float32)[None, :], particle_values], axis=0)
    outgoing = pack_rows(packed, target_dev, devices_all, capacity)
    incoming = lax.all_to_all(outgoing, ("bx", "by"), split_axis=0, concat_axis=0, tiled=True)
    painted = paint_rows(incoming)
    layers = ((weight_in, 1), (weight_mid, 2), (weight_out, 1))
    current = extended(painted, (("bx", 2), ("by", 3)), 4)
    for weight, spacing in layers:
        current = convolve(current, weight, spacing)
    return transform(lax.all_to_all(current, "bx", split_axis=1, concat_axis=2, tiled=True))


def solution(mesh):
    placed = (P(None, ("bx", "by")), P(("bx", "by"), None), P(("bx", "by")), P(), P(), P())
    return jax.shard_map(
        on_device,
        mesh=mesh,
        in_specs=placed,
        out_specs=P(None, None, "bx", None, "by"),
        check_vma=False,
    )
```

profile of v0, /device:TPU:0, one launch (start us, length us, event | category | flops | bytes accessed | tf_op | source)
XLA Modules:
  0.0 450.5 jit_solution(7217518934893136089)
XLA Ops:
  3.6 11.6 %while.26 = (s32[]{:T(128)}, f32[32,512]{1,0:T(8,128)S(1)}, bf16[2,1024,32]{1,2,0:T(8,128)(2,1)S(1)}, f32[2,4,1024]{2,1,0:T(4,128)S(1)}, f32[2,32]{1,0:T(2,128)S(1)}, /*index=5*/s32[]{:T(128)}, s32[]{:T(128)}) while((s32[]{:T(128)}, f32[32,512]{1,0:T(8,128)S(1)}, bf16[2,1024,32]{1,2,0:T(8,128)(2,1)S(1)}, ...), condition=%wide.region_4.5_spmd.clone, body=%wide.region_2.4_spmd.clone.sunk | while | flops 271482880 | bytes 5670371 | solution.py:95
  15.8 7.3 %all-to-all-start = ((f32[32,4,128]{2,1,0:T(4,128)}), f32[32,4,128]{2,1,0:T(4,128)S(1)}, u32[]{:S(2)}, u32[]{:S(2)}) async-start(f32[32,4,128]{2,1,0:T(4,128)} %reshape.112), calls=%async_computation | async-start | bytes 131072 | tf_op jit(solution)/shard_map/all_to_all | solution.py:137
  23.1 7.5 %all-to-all-done = f32[32,4,128]{2,1,0:T(4,128)S(1)} async-done(((f32[32,4,128]{2,1,0:T(4,128)}), f32[32,4,128]{2,1,0:T(4,128)S(1)}, u32[]{:S(2)}, u32[]{:S(2)}) %all-to-all-start) | async-done | bytes 65568 | tf_op jit(solution)/shard_map/all_to_all | solution.py:137
  56.3 7.8 %fusion.81 = bf16[9,16,16,136]{3,0,2,1:T(8,128)(2,1)S(1)} fusion(bf16[3,16,16,4]{3,0,2,1:T(4,128)(2,1)S(1)} %collective-permute-done.3, bf16[3,16,16,4]{3,0,2,1:T(4,128)(2,1)S(1)} %collective-permute-done.2, bf16[3,16,4,128]{3,0,2,1:T(4,128)(2,1)S(1)} %collective-permute-done.1, bf16[3,16,8,128]{3,0,2,1:T(4,128)(2,1)S(1)} %bitcast.285, ...), kind=kLoop, calls=%fused_computation.86 | loop fusion | flops 10653696 | bytes 1227264 | tf_op jit(solution)/shard_map/concatenate | solution.py:32
  64.1 7.3 %fusion.101 = f32[16,14,134,64]{2,3,1,0:T(8,128)} fusion(bf16[9,16,16,136]{3,0,2,1:T(8,128)(2,1)S(1)} %fusion.81, bf16[1,1,64,9]{2,1,3,0:T(2,128)(2,1)S(1)} %get-tuple-element.205), kind=kOutput, calls=%fused_computation.113 | convolution fusion | flops 34578432 | bytes 9523712 | tf_op jit(solution)/shard_map/oc,czxy->ozxy/dot_general | solution.py:40
  71.4 7.3 %fusion.87 = f32[16,14,134,64]{2,3,1,0:T(8,128)} fusion(bf16[9,16,16,136]{3,0,2,1:T(8,128)(2,1)S(1)} %fusion.81, bf16[1,1,64,9]{2,1,3,0:T(2,128)(2,1)S(1)} %get-tuple-element.198), kind=kOutput, calls=%fused_computation.99 | convolution fusion | flops 34578432 | bytes 9523712 | tf_op jit(solution)/shard_map/oc,czxy->ozxy/dot_general | solution.py:40
  86.0 7.3 %fusion.91 = f32[16,14,134,64]{2,3,1,0:T(8,128)} fusion(bf16[9,16,16,136]{3,0,2,1:T(8,128)(2,1)S(1)} %fusion.81, bf16[1,1,64,9]{2,1,3,0:T(2,128)(2,1)S(1)} %get-tuple-element.200), kind=kOutput, calls=%fused_computation.103 | convolution fusion | flops 34578432 | bytes 9523712 | tf_op jit(solution)/shard_map/oc,czxy->ozxy/dot_general | solution.py:40
  107.8 19.6 %fusion.97 = f32[16,14,134,64]{2,3,1,0:T(8,128)} fusion(bf16[9,16,16,136]{3,0,2,1:T(8,128)(2,1)S(1)} %fusion.81, bf16[1,1,64,9]{2,1,3,0:T(2,128)(2,1)S(1)} %get-tuple-element.203), kind=kOutput, calls=%fused_computation.109 | convolution fusion | flops 34578432 | bytes 9523712 | tf_op jit(solution)/shard_map/oc,czxy->ozxy/dot_general | solution.py:40
  134.6 39.4 %fusion.55 = bf16[64,16,14,134]{3,0,2,1:T(8,128)(2,1)} fusion(f32[16,14,134,64]{2,3,1,0:T(8,128)} %fusion.87, f32[16,14,134,64]{2,3,1,0:T(8,128)} %fusion.89, f32[16,14,134,64]{2,3,1,0:T(8,128)} %fusion.91, f32[16,14,134,64]{2,3,1,0:T(8,128)} %fusion.93, f32[16,14,134,64]{2,3,1,0:T(8,128)} %fusion.95, f32[16,14,134,64]{2,3,1,0:T(8,128)} %fusion.97, ...), kind=kOutput, calls=%fused_computation.61 | convolution fusion | flops 57630720 | bytes 67154432 | tf_op jit(solution)/shard_map/oc,czxy->ozxy/dot_general | solution.py:40
  174.0 9.8 %fusion.150 = (bf16[64,14,14,134]{3,0,2,1:T(8,128)(2,1)}, bf16[64,14,14,134]{3,0,2,1:T(8,128)(2,1)}) fusion(bf16[64,16,14,134]{3,0,2,1:T(8,128)(2,1)} %fusion.55), kind=kLoop, calls=%fused_computation.182 | loop fusion | bytes 13447168 | tf_op jit(solution)/shard_map/jit(_roll_static)/slice | solution.py:33
  185.4 14.7 %maximum_maximum_fusion = bf16[192,16,14,134]{3,0,2,1:T(8,128)(2,1)} fusion(bf16[64,2,14,134]{3,0,2,1:T(8,128)(2,1)S(1)} %get-tuple-element.184, bf16[64,14,14,134]{3,0,2,1:T(8,128)(2,1)} %get-tuple-element.186, bf16[64,16,14,134]{3,0,2,1:T(8,128)(2,1)} %fusion.55, bf16[64,14,14,134]{3,0,2,1:T(8,128)(2,1)} %get-tuple-element.185, ...), kind=kLoop, calls=%fused_computation.41 | loop fusion | flops 57630720 | bytes 23052288 | tf_op jit(solution)/shard_map/concatenate | solution.py:32
  200.1 14.2 %fusion.37 = f32[16,10,130,64]{2,3,1,0:T(8,128)} fusion(bf16[192,16,14,134]{3,0,2,1:T(8,128)(2,1)} %maximum_maximum_fusion, bf16[3,3,64,192]{3,2,1,0:T(8,128)(2,1)S(1)} %copy-done.3), kind=kOutput, calls=%fused_computation.42 | convolution fusion | flops 511180800 | bytes 21086208 | tf_op jit(solution)/shard_map/oc,czxy->ozxy/dot_general | solution.py:40
  214.2 14.2 %fusion.39 = f32[16,10,130,64]{2,3,1,0:T(8,128)} fusion(bf16[192,16,14,134]{3,0,2,1:T(8,128)(2,1)} %maximum_maximum_fusion, bf16[3,3,64,192]{3,2,1,0:T(8,128)(2,1)S(1)} %copy-done.3), kind=kOutput, calls=%fused_computation.44 | convolution fusion | flops 511180800 | bytes 21086208 | tf_op jit(solution)/shard_map/oc,czxy->ozxy/dot_general | solution.py:40
  228.4 12.7 %fusion.41 = f32[16,10,130,64]{2,3,1,0:T(8,128)} fusion(bf16[192,16,14,134]{3,0,2,1:T(8,128)(2,1)} %maximum_maximum_fusion, bf16[3,3,64,192]{3,2,1,0:T(8,128)(2,1)S(1)} %copy-done.3), kind=kOutput, calls=%fused_computation.46 | convolution fusion | flops 511180800 | bytes 21086208 | tf_op jit(solution)/shard_map/oc,czxy->ozxy/dot_general | solution.py:40
  241.1 14.2 %fusion.43 = f32[16,10,130,64]{2,3,1,0:T(8,128)} fusion(bf16[192,16,14,134]{3,0,2,1:T(8,128)(2,1)} %maximum_maximum_fusion, bf16[3,3,64,192]{3,2,1,0:T(8,128)(2,1)S(1)} %copy-done.3), kind=kOutput, calls=%fused_computation.48 | convolution fusion | flops 511180800 | bytes 21086208 | tf_op jit(solution)/shard_map/oc,czxy->ozxy/dot_general | solution.py:40
  255.3 14.1 %fusion.45 = f32[16,10,130,64]{2,3,1,0:T(8,128)} fusion(bf16[192,16,14,134]{3,0,2,1:T(8,128)(2,1)} %maximum_maximum_fusion, bf16[3,3,64,192]{3,2,1,0:T(8,128)(2,1)S(1)} %copy-done.3), kind=kOutput, calls=%fused_computation.50 | convolution fusion | flops 511180800 | bytes 21086208 | tf_op jit(solution)/shard_map/oc,czxy->ozxy/dot_general | solution.py:40
  269.5 12.5 %fusion.47 = f32[16,10,130,64]{2,3,1,0:T(8,128)} fusion(bf16[192,16,14,134]{3,0,2,1:T(8,128)(2,1)} %maximum_maximum_fusion, bf16[3,3,64,192]{3,2,1,0:T(8,128)(2,1)S(1)} %copy-done.3), kind=kOutput, calls=%fused_computation.52 | convolution fusion | flops 511180800 | bytes 21086208 | tf_op jit(solution)/shard_map/oc,czxy->ozxy/dot_general | solution.py:40
  282.0 14.2 %fusion.49 = f32[16,10,130,64]{2,3,1,0:T(8,128)} fusion(bf16[192,16,14,134]{3,0,2,1:T(8,128)(2,1)} %maximum_maximum_fusion, bf16[3,3,64,192]{3,2,1,0:T(8,128)(2,1)S(1)} %copy-done.3), kind=kOutput, calls=%fused_computation.54 | convolution fusion | flops 511180800 | bytes 21086208 | tf_op jit(solution)/shard_map/oc,czxy->ozxy/dot_general | solution.py:40
  296.2 14.1 %fusion.51 = f32[16,10,130,64]{2,3,1,0:T(8,128)} fusion(bf16[192,16,14,134]{3,0,2,1:T(8,128)(2,1)} %maximum_maximum_fusion, bf16[3,3,64,192]{3,2,1,0:T(8,128)(2,1)S(1)} %copy-done.3), kind=kOutput, calls=%fused_computation.56 | convolution fusion | flops 511180800 | bytes 21086208 | tf_op jit(solution)/shard_map/oc,czxy->ozxy/dot_general | solution.py:40
  310.3 34.1 %fusion.56 = bf16[64,16,10,130]{3,0,2,1:T(8,128)(2,1)} fusion(f32[16,10,130,64]{2,3,1,0:T(8,128)} %fusion.37, f32[16,10,130,64]{2,3,1,0:T(8,128)} %fusion.39, f32[16,10,130,64]{2,3,1,0:T(8,128)} %fusion.41, f32[16,10,130,64]{2,3,1,0:T(8,128)} %fusion.43, f32[16,10,130,64]{2,3,1,0:T(8,128)} %fusion.45, f32[16,10,130,64]{2,3,1,0:T(8,128)} %fusion.47, ...), kind=kOutput, calls=%fused_computation.63 | convolution fusion | flops 527155200 | bytes 102309888 | tf_op jit(solution)/shard_map/oc,czxy->ozxy/dot_general | solution.py:40
  344.4 9.8 %fusion.152 = (bf16[64,15,10,130]{3,0,2,1:T(8,128)(2,1)}, bf16[64,15,10,130]{3,0,2,1:T(8,128)(2,1)}) fusion(bf16[64,16,10,130]{3,0,2,1:T(8,128)(2,1)} %fusion.56), kind=kLoop, calls=%fused_computation.184 | loop fusion | bytes 9984000 | tf_op jit(solution)/shard_map/jit(_roll_static)/slice | solution.py:33
  354.3 10.1 %maximum_maximum_fusion.1 = bf16[192,16,10,130]{3,0,2,1:T(8,128)(2,1)S(1)} fusion(bf16[64,1,10,130]{3,0,2,1:T(8,128)(2,1)S(1)} %get-tuple-element.188, bf16[64,15,10,130]{3,0,2,1:T(8,128)(2,1)} %get-tuple-element.190, bf16[64,16,10,130]{3,0,2,1:T(8,128)(2,1)S(1)} %copy-done.1, bf16[64,15,10,130]{3,0,2,1:T(8,128)(2,1)} %get-tuple-element.189, ...), kind=kLoop, calls=%fused_computation.60 | loop fusion | flops 39936000 | bytes 15974400 | tf_op jit(solution)/shard_map/concatenate | solution.py:32
  398.3 15.9 %fusion.75 = bf16[64,16,8,128]{3,0,2,1:T(8,128)(2,1)} fusion(f32[16,8,128,64]{2,3,1,0:T(8,128)} %fusion.57, f32[16,8,128,64]{2,3,1,0:T(8,128)} %fusion.59, f32[16,8,128,64]{2,3,1,0:T(8,128)} %fusion.61, f32[16,8,128,64]{2,3,1,0:T(8,128)} %fusion.63, f32[16,8,128,64]{2,3,1,0:T(8,128)} %fusion.65, f32[16,8,128,64]{2,3,1,0:T(8,128)} %fusion.67, ...), kind=kOutput, calls=%fused_computation.82 | convolution fusion | flops 415236096 | bytes 41975808 | tf_op jit(solution)/shard_map/oc,czxy->ozxy/dot_general | solution.py:40
  417.9 26.4 %all-to-all-done.1 = bf16[64,16,8,128]{3,0,2,1:T(8,128)(2,1)S(1)} async-done(((bf16[64,16,8,128]{3,0,2,1:T(8,128)(2,1)}), bf16[64,16,8,128]{3,0,2,1:T(8,128)(2,1)S(1)}, u32[]{:S(2)}, u32[]{:S(2)}) %all-to-all-start.1) | async-done | bytes 2097184 | tf_op jit(solution)/shard_map/all_to_all | solution.py:143
  (87 shorter events, 120.0 us)
Async XLA Ops:
  15.8 14.8 %all-to-all-start = ((f32[32,4,128]{2,1,0:T(4,128)}), f32[32,4,128]{2,1,0:T(4,128)S(1)}, u32[]{:S(2)}, u32[]{:S(2)}) async-start(f32[32,4,128]{2,1,0:T(4,128)} %reshape.112), calls=%async_computation | async-start | bytes 131072 | tf_op jit(solution)/shard_map/all_to_all | solution.py:137
  30.6 15.0 %copy-start.4 = (bf16[3,3,64,9]{2,1,3,0:T(4,128)(2,1)S(1)}, bf16[3,3,64,9]{2,1,3,0:T(4,128)(2,1)}, u32[]{:S(2)}) copy-start(bf16[3,3,64,9]{2,1,3,0:T(4,128)(2,1)} %param.13) | copy-start | bytes 31108
  35.9 5.3 %collective-permute-start = (bf16[3,16,4,128]{3,0,2,1:T(4,128)(2,1)S(1)}, bf16[3,16,4,128]{3,0,2,1:T(4,128)(2,1)S(1)}, u32[]{:S(2)}, u32[]{:S(2)}) collective-permute-start(bf16[3,16,4,128]{3,0,2,1:T(4,128)(2,1)S(1)} %get-tuple-element.195), channel_id=1, source_target_pairs={{0,4},{4,8},{8,12},{12,16},{16,20},{20,24},{24,28},{28,0},{1,5},{5... | collective-permute-start | bytes 147464 | tf_op jit(solution)/shard_map/ppermute | solution.py:20
  36.0 5.3 %collective-permute-start.1 = (bf16[3,16,4,128]{3,0,2,1:T(4,128)(2,1)S(1)}, bf16[3,16,4,128]{3,0,2,1:T(4,128)(2,1)S(1)}, u32[]{:S(2)}, u32[]{:S(2)}) collective-permute-start(bf16[3,16,4,128]{3,0,2,1:T(4,128)(2,1)S(1)} %get-tuple-element.196), channel_id=1, source_target_pairs={{4,0},{8,4},{12,8},{16,12},{20,16},{24,20},{28,24},{0,28},{5,1},{9... | collective-permute-start | bytes 147464 | tf_op jit(solution)/shard_map/ppermute | solution.py:22
  41.7 11.1 %collective-permute-start.2 = (bf16[3,16,16,4]{3,0,2,1:T(4,128)(2,1)S(1)}, bf16[3,16,16,4]{3,0,2,1:T(4,128)(2,1)S(1)}, u32[]{:S(2)}, u32[]{:S(2)}) collective-permute-start(bf16[3,16,16,4]{3,0,2,1:T(4,128)(2,1)S(1)} %get-tuple-element.193), channel_id=1, source_target_pairs={{0,1},{1,2},{2,3},{3,0},{4,5},{5,6},{6,7},{7,4},{8,9},{9,10},{10,1... | collective-permute-start | bytes 18440 | tf_op jit(solution)/shard_map/ppermute | solution.py:20
  41.9 13.3 %collective-permute-start.3 = (bf16[3,16,16,4]{3,0,2,1:T(4,128)(2,1)S(1)}, bf16[3,16,16,4]{3,0,2,1:T(4,128)(2,1)S(1)}, u32[]{:S(2)}, u32[]{:S(2)}) collective-permute-start(bf16[3,16,16,4]{3,0,2,1:T(4,128)(2,1)S(1)} %get-tuple-element.194), channel_id=1, source_target_pairs={{1,0},{2,1},{3,2},{0,3},{5,4},{6,5},{7,6},{4,7},{9,8},{10,9},{11,1... | collective-permute-start | bytes 18440 | tf_op jit(solution)/shard_map/ppermute | solution.py:22
  185.4 14.7 %copy-start.3 = (bf16[3,3,64,192]{3,2,1,0:T(8,128)(2,1)S(1)}, bf16[3,3,64,192]{3,2,1,0:T(8,128)(2,1)}, u32[]{:S(2)}) copy-start(bf16[3,3,64,192]{3,2,1,0:T(8,128)(2,1)} %param.14) | copy-start | bytes 663556
  344.4 9.8 %copy-start.1 = (bf16[64,16,10,130]{3,0,2,1:T(8,128)(2,1)S(1)}, bf16[64,16,10,130]{3,0,2,1:T(8,128)(2,1)}, u32[]{:S(2)}) copy-start(bf16[64,16,10,130]{3,0,2,1:T(8,128)(2,1)} %fusion.56) | copy-start | bytes 7987204
  354.3 10.2 %copy-start.2 = (bf16[3,3,64,192]{3,2,1,0:T(8,128)(2,1)S(1)}, bf16[3,3,64,192]{3,2,1,0:T(8,128)(2,1)}, u32[]{:S(2)}) copy-start(bf16[3,3,64,192]{3,2,1,0:T(8,128)(2,1)} %param.15) | copy-start | bytes 663556
  364.4 29.5 %copy-start = (bf16[192,16,10,130]{3,0,2,1:T(8,128)(2,1)}, bf16[192,16,10,130]{3,0,2,1:T(8,128)(2,1)S(1)}, u32[]{:S(2)}) copy-start(bf16[192,16,10,130]{3,0,2,1:T(8,128)(2,1)S(1)} %maximum_maximum_fusion.1) | copy-start | bytes 23961604
  414.2 30.2 %all-to-all-start.1 = ((bf16[64,16,8,128]{3,0,2,1:T(8,128)(2,1)}), bf16[64,16,8,128]{3,0,2,1:T(8,128)(2,1)S(1)}, u32[]{:S(2)}, u32[]{:S(2)}) async-start(bf16[64,16,8,128]{3,0,2,1:T(8,128)(2,1)} %fusion.75), calls=%async_computation.1 | async-start | bytes 4194304 | tf_op jit(solution)/shard_map/all_to_all | solution.py:143
where the time goes:
time: 458 us; the launch traced here: 451 us
  matrix products  313 us (68%)
  waiting for transfers between devices  46 us (10%)
  other arithmetic  45.9 us (10%)
  local copies, waits for them, and re-layouts  26.9 us (6%)
  starting transfers between devices  17.5 us (4%)
    dot_general x27, matrix products, convolve(): jnp.einsum('oc,czxy->ozxy', weight[step_x, step_y], window, preferred_ele...  304 us
    concatenate x3, other arithmetic, convolve(): jnp.concatenate([jnp.roll(widened, spacing, axis=1), widened, jnp.roll(wi...  32.6 us
    all_to_all x1, waiting for transfers between devices, on_device(): lax.all_to_all(current, 'bx', split_axis=1, concat_axis=2, tiled=True)  26.4 us
    slice x5, local copies, waits for them, and re-layouts, convolve(): jnp.roll(widened, spacing, axis=1)  21.7 us
    ppermute x2, waiting for transfers between devices, extended(): lax.ppermute(tail, axis, [(i, (i + 1) % count) for i in range(count)])  9.81 us
  transfers between devices with their start and end apart: 6, of which 5 were waited for; matrix products, arithmetic and copies ran while one was open for 0% of the time, Pallas kernels for 0%

commit v1 on v0

v1 whole, which is shorter than its diff:
```python
import functools
import math

import jax
import jax.numpy as jnp
import numpy as np
from jax import lax
from jax.experimental import pallas as pl
from jax.experimental.pallas import tpu as pltpu
from jax.sharding import PartitionSpec as P

CELL_X = 8
CELL_Y = 128
CELL_Z = 16
CHANNELS = 64
COMPS = 3
HALO = 4
ROW = CELL_Y + 2 * HALO
NT = (((1,), (1,)), ((), ()))


def twiddle_table(count):
    position = jnp.arange(count, dtype=jnp.int32)
    phase = position[:, None] * position[None, :] % count
    angle = phase.astype(jnp.float32) * (2.0 * math.pi / count)
    factor = 1.0 / math.sqrt(count)
    return jnp.stack([jnp.cos(angle) * factor, -jnp.sin(angle) * factor]).astype(jnp.bfloat16)


def three_parts(value):
    high = value.astype(jnp.bfloat16).astype(jnp.float32)
    rest = value - high
    middle = rest.astype(jnp.bfloat16).astype(jnp.float32)
    return high, middle, rest - middle


def pack_kernel(dest_ref, cell_ref, value_ref, out_ref):
    bricks, _, capacity = out_ref.shape
    rows = dest_ref.shape[1]
    block = min(256, rows)
    upper = (
        lax.broadcasted_iota(jnp.int32, (block, block), 0)
        < lax.broadcasted_iota(jnp.int32, (block, block), 1)
    ).astype(jnp.float32).astype(jnp.bfloat16)
    brick_ids = lax.broadcasted_iota(jnp.int32, (bricks, block), 0)
    slot_ids = lax.broadcasted_iota(jnp.int32, (capacity, block), 0)
    start = jnp.zeros((bricks, 1), jnp.float32)
    total = jnp.zeros((12 * bricks, capacity), jnp.float32)
    for number in range(rows // block):
        span = slice(number * block, (number + 1) * block)
        hot = (brick_ids == dest_ref[:, span]).astype(jnp.float32)
        before = jnp.dot(hot.astype(jnp.bfloat16), upper, preferred_element_type=jnp.float32)
        slot = jnp.sum(hot * (before + start), axis=0, keepdims=True).astype(jnp.int32)
        start = start + jnp.sum(hot, axis=1, keepdims=True)
        slot_hot = (slot_ids == slot).astype(jnp.float32).astype(jnp.bfloat16)
        data = [cell_ref[:, span].astype(jnp.float32)]
        data += [value_ref[f : f + 1, span] for f in range(COMPS)]
        spread = [hot * part for row in data for part in three_parts(row)]
        total = total + lax.dot_general(
            jnp.concatenate(spread, axis=0).astype(jnp.bfloat16),
            slot_hot,
            NT,
            preferred_element_type=jnp.float32,
        )
    for w in range(COMPS + 1):
        parts = [total[(3 * w + i) * bricks : (3 * w + i + 1) * bricks] for i in range(3)]
        out_ref[:, w, :] = (parts[0] + parts[1]) + parts[2]


def pack(destination, cells, values, devices_all, capacity):
    return pl.pallas_call(
        pack_kernel,
        out_shape=jax.ShapeDtypeStruct((devices_all, COMPS + 1, capacity), jnp.float32),
        in_specs=[pl.BlockSpec(memory_space=pltpu.VMEM)] * 3,
        out_specs=pl.BlockSpec(memory_space=pltpu.VMEM),
        compiler_params=pltpu.CompilerParams(vmem_limit_bytes=48 * 2**20),
        name="pack",
    )(destination, cells, values)


def paint_kernel(cell_ref, value_ref, out_ref):
    rows = cell_ref.shape[1]
    block = min(512, rows)
    lines = CELL_Z * CELL_X
    high_ids = lax.broadcasted_iota(jnp.int32, (lines, block), 0)
    total = jnp.zeros((lines, 9 * CELL_Y), jnp.float32)
    for number in range(rows // block):
        span = slice(number * block, (number + 1) * block)
        cell = cell_ref[:, span].astype(jnp.int32)
        high_hot = (high_ids == cell // CELL_Y).astype(jnp.float32).astype(jnp.bfloat16)
        low_hot = (high_ids == cell % CELL_Y).astype(jnp.float32)
        spread = []
        for f in range(COMPS):
            for part in three_parts(value_ref[f : f + 1, span]):
                spread.append((low_hot * part).astype(jnp.bfloat16))
        total = total + lax.dot_general(
            high_hot, jnp.concatenate(spread, axis=0), NT, preferred_element_type=jnp.float32
        )
    for f in range(COMPS):
        parts = [total[:, (3 * f + i) * CELL_Y : (3 * f + i + 1) * CELL_Y] for i in range(3)]
        out_ref[:, f * CELL_Y : (f + 1) * CELL_Y] = (
            (parts[0] + parts[1]) + parts[2]
        ).astype(jnp.bfloat16)


def paint(cells, values):
    lines = CELL_Z * CELL_X
    return pl.pallas_call(
        paint_kernel,
        out_shape=jax.ShapeDtypeStruct((lines, COMPS * CELL_Y), jnp.bfloat16),
        in_specs=[pl.BlockSpec(memory_space=pltpu.VMEM)] * 2,
        out_specs=pl.BlockSpec(memory_space=pltpu.VMEM),
        compiler_params=pltpu.CompilerParams(vmem_limit_bytes=48 * 2**20),
        name="paint",
    )(cells, values)


def up(number):
    return -(-number // 128) * 128


WIDE_0 = up((CELL_X + 8) * ROW)
WIDE_1 = up((CELL_X + 6) * ROW)
WIDE_2 = up((CELL_X + 2) * ROW)
WIDE_3 = up(CELL_X * ROW)
HELD_0 = WIDE_0 + 128
HELD_1 = WIDE_1 + 128
HELD_2 = WIDE_2 + 128
TAPS_1 = 512


def chunks(width):
    return [(at, min(256, width - at)) for at in range(0, width, 256)]


def window(load, offset, size):
    first, turn = offset // 128 * 128, offset % 128
    if turn == 0:
        return load(first, size)
    return pltpu.roll(load(first, size + 128), size + 128 - turn, 1)[:, :size]


def leaky(value):
    return jnp.maximum(value, 0.1 * value)


def conv_kernel(painted_ref, pick_ref, w1_ref, w2_ref, w3_ref, out_ref, big, first, second, total):
    depth = CELL_Z

    def spread_weight(z, carry):
        rows = pl.ds(pl.multiple_of(z * CHANNELS, CHANNELS), CHANNELS)
        big[rows, :] = jnp.dot(
            w1_ref[...], pick_ref[z], preferred_element_type=jnp.float32
        ).astype(jnp.bfloat16)
        return carry

    lax.fori_loop(0, depth, spread_weight, 0)
    planes = painted_ref.shape[0]
    for z in range(depth):
        first[z, :, WIDE_1:] = jnp.zeros((CHANNELS, HELD_1 - WIDE_1), jnp.bfloat16)
        second[z, :, WIDE_2:] = jnp.zeros((CHANNELS, HELD_2 - WIDE_2), jnp.bfloat16)
    for at, size in chunks(WIDE_1):
        pieces = [
            window(lambda a, n: painted_ref[:, a : a + n], at + tx * ROW + ty, size)
            for tx in range(3)
            for ty in range(3)
        ]
        pieces.append(jnp.zeros((TAPS_1 - 9 * planes, size), jnp.bfloat16))
        taps = jnp.concatenate(pieces, axis=0)

        def four(g, carry):
            rows = pl.ds(pl.multiple_of(g * 4 * CHANNELS, 4 * CHANNELS), 4 * CHANNELS)
            value = leaky(jnp.dot(big[rows, :], taps, preferred_element_type=jnp.float32))
            value = value.astype(jnp.bfloat16)
            for i in range(4):
                first[g * 4 + i, :, at : at + size] = value[i * CHANNELS : (i + 1) * CHANNELS]
            return carry

        for g in range(depth // 4):
            four(g, 0)

    def layer(source, weight_ref, spacing, width):
        def clear(z, carry):
            total[z, :, :width] = jnp.zeros((CHANNELS, width), jnp.float32)
            return carry

        lax.fori_loop(0, depth, clear, 0)

        def plane(z, carry):
            for at, size in chunks(width):
                taps = jnp.concatenate(
                    [
                        window(
                            lambda a, n: source[z, :, a : a + n],
                            at + (tx * ROW + ty) * spacing,
                            size,
                        )
                        for tx in range(3)
                        for ty in range(3)
                    ],
                    axis=0,
                )
                value = jnp.dot(weight_ref[...], taps, preferred_element_type=jnp.float32)
                for tz in range(3):
                    to = lax.rem(z - (tz - 1) * spacing + depth, depth)
                    total[to, :, at : at + size] += value[tz * CHANNELS : (tz + 1) * CHANNELS]
            return carry

        lax.fori_loop(0, depth, plane, 0)

    layer(first, w2_ref, 2, WIDE_2)

    def finish_second(z, carry):
        second[z, :, :WIDE_2] = leaky(total[z]).astype(jnp.bfloat16)
        return carry

    lax.fori_loop(0, depth, finish_second, 0)
    layer(second, w3_ref, 1, WIDE_3)

    def finish_third(z, carry):
        value = leaky(total[z, :, :WIDE_3])
        for x in range(CELL_X):
            out_ref[z, x] = value[:, x * ROW : x * ROW + CELL_Y].astype(jnp.bfloat16)
        return carry

    lax.fori_loop(0, depth, finish_third, 0)


def pick_table():
    table = np.zeros((CELL_Z, 9, 3, COMPS, TAPS_1), np.float32)
    for z in range(CELL_Z):
        for tap in range(9):
            for tz in range(3):
                for i in range(COMPS):
                    plane = (z + tz - 1) % CELL_Z
                    table[z, tap, tz, i, tap * CELL_Z * COMPS + plane * COMPS + i] = 1
    return table.reshape(CELL_Z, 27 * COMPS, TAPS_1)


def convolve_all(painted, weight_in, weight_mid, weight_out):
    pick = jnp.asarray(pick_table(), jnp.bfloat16)
    w1 = jnp.transpose(weight_in, (2, 0, 1, 3)).reshape(CHANNELS, 27 * COMPS)

    def arranged(weight):
        split = weight.reshape(3, 3, CHANNELS, 3, CHANNELS)
        return jnp.transpose(split, (3, 2, 0, 1, 4)).reshape(3 * CHANNELS, 9 * CHANNELS)

    return pl.pallas_call(
        conv_kernel,
        out_shape=jax.ShapeDtypeStruct((CELL_Z, CELL_X, CHANNELS, CELL_Y), jnp.bfloat16),
        in_specs=[pl.BlockSpec(memory_space=pltpu.VMEM)] * 5,
        out_specs=pl.BlockSpec(memory_space=pltpu.VMEM),
        scratch_shapes=[
            pltpu.VMEM((CELL_Z * CHANNELS, TAPS_1), jnp.bfloat16),
            pltpu.VMEM((CELL_Z, CHANNELS, HELD_1), jnp.bfloat16),
            pltpu.VMEM((CELL_Z, CHANNELS, HELD_2), jnp.bfloat16),
            pltpu.VMEM((CELL_Z, CHANNELS, WIDE_2), jnp.float32),
        ],
        compiler_params=pltpu.CompilerParams(vmem_limit_bytes=48 * 2**20),
        name="convolutions",
    )(painted, pick, w1, arranged(weight_mid), arranged(weight_out))


def extended(cells, axis, dim):
    count = lax.axis_size(axis)
    size = cells.shape[dim]
    head = lax.slice_in_dim(cells, 0, HALO, axis=dim)
    tail = lax.slice_in_dim(cells, size - HALO, size, axis=dim)
    return jnp.concatenate(
        [
            lax.ppermute(tail, axis, [(i, (i + 1) % count) for i in range(count)]),
            cells,
            lax.ppermute(head, axis, [((i + 1) % count, i) for i in range(count)]),
        ],
        axis=dim,
    )


def on_device(particle_values, destination, cell_index, weight_in, weight_mid, weight_out):
    devices_all = lax.axis_size("bx") * lax.axis_size("by")
    rows_here = cell_index.shape[0]
    capacity = 2 * rows_here // devices_all
    outgoing = pack(
        destination.reshape(1, rows_here),
        cell_index.reshape(1, rows_here),
        particle_values,
        devices_all,
        capacity,
    )
    incoming = lax.all_to_all(outgoing, ("bx", "by"), split_axis=0, concat_axis=0, tiled=True)
    incoming = jnp.transpose(incoming, (1, 0, 2)).reshape(COMPS + 1, devices_all * capacity)
    painted = paint(incoming[:1], incoming[1:])
    cells = painted.reshape(CELL_Z, CELL_X, COMPS, CELL_Y)
    cells = extended(extended(cells, "bx", 1), "by", 3)
    cells = jnp.transpose(cells, (0, 2, 1, 3)).reshape(CELL_Z * COMPS, (CELL_X + 8) * ROW)
    cells = jnp.pad(cells, ((0, 0), (0, HELD_0 - cells.shape[1])))
    third = convolve_all(cells, weight_in, weight_mid, weight_out)
    moved = lax.all_to_all(third, "bx", split_axis=0, concat_axis=1, tiled=True)
    twiddle = twiddle_table(moved.shape[1])
    return jnp.einsum(
        "tkx,zxcy->tczky", twiddle, moved, preferred_element_type=jnp.float32
    ).astype(jnp.bfloat16)


def solution(mesh):
    placed = (P(None, ("bx", "by")), P(("bx", "by"), None), P(("bx", "by")), P(), P(), P())
    return jax.shard_map(
        on_device,
        mesh=mesh,
        in_specs=placed,
        out_specs=P(None, None, "bx", None, "by"),
        check_vma=False,
    )
```

time: 458 us -> 111 us (0.24); the launches traced: 451 us -> 110 us
  matrix products: 313 us -> 1.93 us
  other arithmetic: 45.9 us -> 1.74 us
  Pallas kernels: 0 us -> 40.1 us
  local copies, waits for them, and re-layouts: 26.9 us -> 9.66 us
  blocking collectives: 0 us -> 14.6 us
  waiting for transfers between devices: 46 us -> 31.6 us
  starting transfers between devices: 17.5 us -> 10.4 us
    dot_general x34 -> x1, matrix products: 313 us -> 1.93 us  [on_device(): jnp.einsum('tkx,zxcy->tczky', twiddle, moved, preferred_element_type=jnp....]
    pallas_call x0 -> x3, Pallas kernels: none -> 40.1 us  [the longest x1 35.5 us: convolve_all(): pl.pallas_call(conv_kernel, out_shape=jax.ShapeDtypeStruct((CELL_Z, CELL_...]
    concatenate x3 -> x0, other arithmetic: 32.6 us -> none  [convolve(): jnp.concatenate([jnp.roll(widened, spacing, axis=1), widened, jnp.roll(wi...]
    slice x10 -> x4, local copies, waits for them, and re-layouts: 22 us -> 0.19 us  [the longest x2 0.16 us: extended(): tail = lax.slice_in_dim(cells, size - HALO, size, axis=dim)]
    all_to_all x0 -> x1, blocking collectives: none -> 14.6 us  [on_device(): lax.all_to_all(outgoing, ('bx', 'by'), split_axis=0, concat_axis=0, tiled...]
    dot_general x4 -> x0, other arithmetic: 8.48 us -> none  [the longest x2 7.75 us: pack_one_block(): jnp.einsum('wp,ps->pws', data_block, slot_hot)]
    all_to_all x2 -> x1, waiting for transfers between devices: 33.9 us -> 26.2 us  [on_device(): moved = lax.all_to_all(third, 'bx', split_axis=0, concat_axis=1, tiled=True)]
    all_to_all x2 -> x1, starting transfers between devices: 10.9 us -> 3.79 us  [on_device(): moved = lax.all_to_all(third, 'bx', split_axis=0, concat_axis=1, tiled=True)]
  transfers between devices with their start and end apart: 6 -> 5, of which waited for: 5 -> 4; matrix products, arithmetic and copies ran while one was open for 0% -> 4% of each run, Pallas kernels for 0% -> 0%
where the time goes in v1:
time: 111 us; the launch traced here: 110 us
  Pallas kernels  40.1 us (36%)
  waiting for transfers between devices  31.6 us (28%)
  blocking collectives  14.6 us (13%)
  starting transfers between devices  10.4 us (9%)
  local copies, waits for them, and re-layouts  9.66 us (9%)
  matrix products  1.93 us (2%)
  other arithmetic  1.74 us (2%)
    pallas_call x1, Pallas kernels, convolve_all(): pl.pallas_call(conv_kernel, out_shape=jax.ShapeDtypeStruct((CELL_Z, CELL_...  35.5 us
    all_to_all x1, waiting for transfers between devices, on_device(): moved = lax.all_to_all(third, 'bx', split_axis=0, concat_axis=1, tiled=True)  26.2 us
    all_to_all x1, blocking collectives, on_device(): lax.all_to_all(outgoing, ('bx', 'by'), split_axis=0, concat_axis=0, tiled...  14.6 us
    ppermute x2, starting transfers between devices, extended(): lax.ppermute(head, axis, [((i + 1) % count, i) for i in range(count)])  6.35 us
    ppermute x2, waiting for transfers between devices, extended(): lax.ppermute(tail, axis, [(i, (i + 1) % count) for i in range(count)])  4.28 us
    all_to_all x1, starting transfers between devices, on_device(): moved = lax.all_to_all(third, 'bx', split_axis=0, concat_axis=1, tiled=True)  3.79 us
    pallas_call x1, Pallas kernels, paint(): pl.pallas_call(paint_kernel, out_shape=jax.ShapeDtypeStruct((lines, COMPS...  3.13 us
    convert_element_type x1, local copies, waits for them, and re-layouts, on_device(): return jnp.einsum('tkx,zxcy->tczky', twiddle, moved, preferred_element_ty...  2.97 us
  transfers between devices with their start and end apart: 5, of which 4 were waited for; matrix products, arithmetic and copies ran while one was open for 4% of the time, Pallas kernels for 0%

profile of v1, /device:TPU:0, one launch (start us, length us, event | category | flops | bytes accessed | tf_op | source)
XLA Modules:
  0.0 110.2 jit_solution(9178942948739978033)
XLA Ops:
  0.0 0.8 copy-done.1
  0.8 0.7 copy-done.2
  1.5 0.7 copy-done.3
  2.2 1.5 %pack.1 = f32[32,4,128]{2,1,0:T(4,128)S(1)} custom-call(s32[1,2048]{1,0:T(1,128)S(1)} %bitcast.41, s32[1,2048]{1,0:T(1,128)S(1)} %bitcast.42, f32[3,2048]{1,0:T(4,128)S(1)} %copy-done.1), custom_call_target="tpu_custom_call" | custom-call | tf_op jit(solution)/shard_map/pack/pallas_call | solution.py:71
  3.7 14.6 %all_to_all.23 = f32[32,4,128]{2,1,0:T(4,128)S(1)} all-to-all(f32[32,4,128]{2,1,0:T(4,128)S(1)} %pack.1), channel_id=1, replica_groups=mesh['bx'=8,'by'=4] {'bx','by'}, dimensions={0} | all-to-all | bytes 131072 | tf_op jit(solution)/shard_map/all_to_all | solution.py:290
  18.3 3.1 %paint.1 = bf16[128,384]{1,0:T(8,128)(2,1)S(1)} custom-call(f32[1,4096]{1,0:T(1,128)S(1)} %slice_bitcast_fusion.1.cell_ref, f32[3,4096]{1,0:T(4,128)S(1)} %slice_bitcast_fusion.value_ref), custom_call_target="tpu_custom_call" | custom-call | tf_op jit(solution)/shard_map/paint/pallas_call | solution.py:108
  21.6 2.6 %collective-permute-start.1 = (bf16[16,4,3,128]{3,1,2,0:T(4,128)(2,1)S(1)}, bf16[16,4,3,128]{3,1,2,0:T(4,128)(2,1)S(1)}, u32[]{:S(2)}, u32[]{:S(2)}) collective-permute-start(bf16[16,4,3,128]{3,1,2,0:T(4,128)(2,1)S(1)} %get-tuple-element.8), channel_id=1, source_target_pairs={{4,0},{8,4},{12,8},{16,12},{20,16},{24,20},{28,24},{0,28},{5,1},{9... | collective-permute-start | bytes 147464 | tf_op jit(solution)/shard_map/ppermute | solution.py:273
  24.2 2.3 %collective-permute-done = bf16[16,4,3,128]{3,1,2,0:T(4,128)(2,1)S(1)} collective-permute-done((bf16[16,4,3,128]{3,1,2,0:T(4,128)(2,1)S(1)}, bf16[16,4,3,128]{3,1,2,0:T(4,128)(2,1)S(1)}, u32[]{:S(2)}, u32[]{:S(2)}) %collective-permute-start) | collective-permute-done | bytes 49184 | tf_op jit(solution)/shard_map/ppermute | solution.py:271
  26.9 3.7 %collective-permute-start.3 = (bf16[16,16,3,4]{3,1,2,0:T(8,128)(2,1)S(1)}, bf16[16,16,3,4]{3,1,2,0:T(8,128)(2,1)}, u32[]{:S(2)}, u32[]{:S(2)}) collective-permute-start(bf16[16,16,3,4]{3,1,2,0:T(8,128)(2,1)S(1)} %get-tuple-element.6), channel_id=1, source_target_pairs={{1,0},{2,1},{3,2},{0,3},{5,4},{6,5},{7,6},{4,7},{9,8},{10,9},{11,1... | collective-permute-start | bytes 18440 | tf_op jit(solution)/shard_map/ppermute | solution.py:273
  30.6 0.8 copy.13
  31.5 0.3 copy.14
  31.8 0.8 copy.15
  32.6 0.4 reshape.113.w2_ref
  33.3 0.8 copy.17
  34.1 0.4 reshape.115.w3_ref
  34.5 2.0 %collective-permute-done.2 = bf16[16,16,3,4]{3,1,2,0:T(8,128)(2,1)} collective-permute-done((bf16[16,16,3,4]{3,1,2,0:T(8,128)(2,1)S(1)}, bf16[16,16,3,4]{3,1,2,0:T(8,128)(2,1)}, u32[]{:S(2)}, u32[]{:S(2)}) %collective-permute-start.2) | collective-permute-done | bytes 6176 | tf_op jit(solution)/shard_map/ppermute | solution.py:271
  36.5 1.1 %collective-permute-done.3 = bf16[16,16,3,4]{3,1,2,0:T(8,128)(2,1)} collective-permute-done((bf16[16,16,3,4]{3,1,2,0:T(8,128)(2,1)S(1)}, bf16[16,16,3,4]{3,1,2,0:T(8,128)(2,1)}, u32[]{:S(2)}, u32[]{:S(2)}) %collective-permute-start.3) | collective-permute-done | bytes 6176 | tf_op jit(solution)/shard_map/ppermute | solution.py:273
  37.6 1.5 %maximum_bitcast_fusion = bf16[16,3,16,136]{3,2,1,0:T(8,128)(2,1)S(1)} fusion(bf16[16,16,3,4]{3,1,2,0:T(8,128)(2,1)} %collective-permute-done.3, bf16[16,4,3,128]{3,1,2,0:T(4,128)(2,1)} %copy-done.6, bf16[16,8,3,128]{3,1,2,0:T(8,128)(2,1)S(1)} %bitcast.40, bf16[16,4,3,128]{3,1,2,0:T(4,128)(2,1)S(1)} %collective-permute-done, ...), kind=kLoop, calls=%fused_computation.3 | loop fusion | flops 1044480 | bytes 417792 | tf_op jit(solution)/shard_map/transpose | solution.py:295
  39.1 0.5 reshape.110
  39.6 35.5 %convolutions.1 = bf16[16,8,64,128]{3,2,1,0:T(8,128)(2,1)} custom-call(bf16[48,2304]{1,0:T(8,128)(2,1)S(1)} %pad.4.painted_ref, bf16[16,81,512]{2,1,0:T(8,128)(2,1)S(1)} %copy-done, bf16[64,81]{1,0:T(8,128)(2,1)S(1)} %copy.18.w1_ref, bf16[192,576]{1,0:T(8,128)(2,1)S(1)} %reshape.113.w2_ref, bf16[192,576]{1,0:T(8,128)(2,1)S(1)} %reshape.115.w3_ref), custom_call_target="tpu_custom_call" | custom-call | tf_op jit(solution)/shard_map/convolutions/pallas_call | solution.py:248
  75.1 3.8 %all-to-all-start.1 = ((bf16[16,8,64,128]{3,2,1,0:T(8,128)(2,1)}), bf16[16,8,64,128]{3,2,1,0:T(8,128)(2,1)S(1)}, u32[]{:S(2)}, u32[]{:S(2)}) async-start(bf16[16,8,64,128]{3,2,1,0:T(8,128)(2,1)} %convolutions.1), calls=%async_computation.1 | async-start | bytes 4194304 | tf_op jit(solution)/shard_map/all_to_all | solution.py:298
  79.1 26.2 %all-to-all-done.1 = bf16[16,8,64,128]{3,2,1,0:T(8,128)(2,1)S(1)} async-done(((bf16[16,8,64,128]{3,2,1,0:T(8,128)(2,1)}), bf16[16,8,64,128]{3,2,1,0:T(8,128)(2,1)S(1)}, u32[]{:S(2)}, u32[]{:S(2)}) %all-to-all-start.1) | async-done | bytes 2097184 | tf_op jit(solution)/shard_map/all_to_all | solution.py:298
  105.3 1.9 %convert_bitcast_fusion = bf16[2,64,2,64,128]{4,3,0,1,2:T(8,128)(2,1)S(1)} fusion(bf16[2,8,8,64,128]{4,3,2,0,1:T(8,128)(2,1)S(1)} %bitcast.43, bf16[1,64,64]{2,1,0:T(8,128)(2,1)S(1)} %get-tuple-element.9, bf16[1,64,64]{2,1,0:T(8,128)(2,1)S(1)} %get-tuple-element.10), kind=kOutput, calls=%fused_computation | convolution fusion | flops 270565376 | bytes 6307840 | tf_op jit(solution)/shard_map/tkx,zxcy->tczky/dot_general | solution.py:300
  107.2 3.0 %copy.20 = bf16[2,64,2,64,128]{4,3,2,1,0:T(8,128)(2,1)} copy(bf16[2,64,2,64,128]{4,3,0,1,2:T(8,128)(2,1)S(1)} %convert_bitcast_fusion) | data formatting | bytes 8388608 | tf_op jit(solution)/shard_map/convert_element_type | solution.py:302
  (24 shorter events, 1.1 us)
Async XLA Ops:
  0.0 0.8 copy-start.1
  0.8 0.7 copy-start.2
  1.5 0.7 copy-start.3
  2.2 29.3 %copy-start.4 = (bf16[3,3,64,192]{3,2,1,0:T(8,128)(2,1)S(1)}, bf16[3,3,64,192]{3,2,1,0:T(8,128)(2,1)}, u32[]{:S(2)}) copy-start(bf16[3,3,64,192]{3,2,1,0:T(8,128)(2,1)} %param.11) | copy-start | bytes 663556
  21.4 11.6 %copy-start.5 = (bf16[3,3,64,192]{3,2,1,0:T(8,128)(2,1)S(1)}, bf16[3,3,64,192]{3,2,1,0:T(8,128)(2,1)}, u32[]{:S(2)}) copy-start(bf16[3,3,64,192]{3,2,1,0:T(8,128)(2,1)} %param.12) | copy-start | bytes 663556
  21.5 5.0 %collective-permute-start = (bf16[16,4,3,128]{3,1,2,0:T(4,128)(2,1)S(1)}, bf16[16,4,3,128]{3,1,2,0:T(4,128)(2,1)S(1)}, u32[]{:S(2)}, u32[]{:S(2)}) collective-permute-start(bf16[16,4,3,128]{3,1,2,0:T(4,128)(2,1)S(1)} %get-tuple-element.7), channel_id=1, source_target_pairs={{0,4},{4,8},{8,12},{12,16},{16,20},{20,24},{24,28},{28,0},{1,5},{5... | collective-permute-start | bytes 147464 | tf_op jit(solution)/shard_map/ppermute | solution.py:271
  21.6 4.9 %collective-permute-start.1 = (bf16[16,4,3,128]{3,1,2,0:T(4,128)(2,1)S(1)}, bf16[16,4,3,128]{3,1,2,0:T(4,128)(2,1)S(1)}, u32[]{:S(2)}, u32[]{:S(2)}) collective-permute-start(bf16[16,4,3,128]{3,1,2,0:T(4,128)(2,1)S(1)} %get-tuple-element.8), channel_id=1, source_target_pairs={{4,0},{8,4},{12,8},{16,12},{20,16},{24,20},{28,24},{0,28},{5,1},{9... | collective-permute-start | bytes 147464 | tf_op jit(solution)/shard_map/ppermute | solution.py:273
  26.5 5.3 %copy-start.6 = (bf16[16,4,3,128]{3,1,2,0:T(4,128)(2,1)}, bf16[16,4,3,128]{3,1,2,0:T(4,128)(2,1)S(1)}, u32[]{:S(2)}) copy-start(bf16[16,4,3,128]{3,1,2,0:T(4,128)(2,1)S(1)} %collective-permute-done.1) | copy-start | bytes 147460
  26.7 9.8 %collective-permute-start.2 = (bf16[16,16,3,4]{3,1,2,0:T(8,128)(2,1)S(1)}, bf16[16,16,3,4]{3,1,2,0:T(8,128)(2,1)}, u32[]{:S(2)}, u32[]{:S(2)}) collective-permute-start(bf16[16,16,3,4]{3,1,2,0:T(8,128)(2,1)S(1)} %get-tuple-element.5), channel_id=1, source_target_pairs={{0,1},{1,2},{2,3},{3,0},{4,5},{5,6},{6,7},{7,4},{8,9},{9,10},{10,1... | collective-permute-start | bytes 18440 | tf_op jit(solution)/shard_map/ppermute | solution.py:271
  26.9 10.7 %collective-permute-start.3 = (bf16[16,16,3,4]{3,1,2,0:T(8,128)(2,1)S(1)}, bf16[16,16,3,4]{3,1,2,0:T(8,128)(2,1)}, u32[]{:S(2)}, u32[]{:S(2)}) collective-permute-start(bf16[16,16,3,4]{3,1,2,0:T(8,128)(2,1)S(1)} %get-tuple-element.6), channel_id=1, source_target_pairs={{1,0},{2,1},{3,2},{0,3},{5,4},{6,5},{7,6},{4,7},{9,8},{10,9},{11,1... | collective-permute-start | bytes 18440 | tf_op jit(solution)/shard_map/ppermute | solution.py:273
  33.3 6.4 %copy-start = (bf16[16,81,512]{2,1,0:T(8,128)(2,1)S(1)}, bf16[16,81,512]{2,1,0:T(8,128)(2,1)}, u32[]{:S(2)}) copy-start(bf16[16,81,512]{2,1,0:T(8,128)(2,1)} %constant.24.clone.pick_ref) | copy-start | bytes 3981316
  75.1 30.2 %all-to-all-start.1 = ((bf16[16,8,64,128]{3,2,1,0:T(8,128)(2,1)}), bf16[16,8,64,128]{3,2,1,0:T(8,128)(2,1)S(1)}, u32[]{:S(2)}, u32[]{:S(2)}) async-start(bf16[16,8,64,128]{3,2,1,0:T(8,128)(2,1)} %convolutions.1), calls=%async_computation.1 | async-start | bytes 4194304 | tf_op jit(solution)/shard_map/all_to_all | solution.py:298

commit v2 on v1

--- a/solution.py
+++ b/solution.py
@@ -144,8 +144,83 @@
     return jnp.maximum(value, 0.1 * value)
 
 
-def conv_kernel(painted_ref, pick_ref, w1_ref, w2_ref, w3_ref, out_ref, big, first, second, total):
+MESH = pl.DeviceIdType.MESH
+PLANES = CELL_Z * COMPS
+
+
+def neighbours(count_x, count_y, me_x, me_y):
+    around = []
+    for dx in (-1, 0, 1):
+        for dy in (-1, 0, 1):
+            if dx or dy:
+                place = (lax.rem(me_x + dx + count_x, count_x), lax.rem(me_y + dy + count_y, count_y))
+                around.append((dx, dy, place))
+    return around
+
+
+def conv_kernel(
+    count_x,
+    count_y,
+    cells_ref,
+    edge_ref,
+    pick_ref,
+    w1_ref,
+    w2_ref,
+    w3_ref,
+    out_ref,
+    side,
+    corner,
+    painted,
+    big,
+    mid,
+    last,
+    first,
+    second,
+    total_2,
+    total_3,
+    third,
+    halo_send,
+    halo_recv,
+    plane_send,
+    plane_recv,
+):
     depth = CELL_Z
+    share = depth // count_x
+    me_x, me_y = lax.axis_index("bx"), lax.axis_index("by")
+    around = neighbours(count_x, count_y, me_x, me_y)
+
+    barrier = pltpu.get_barrier_semaphore()
+    for step in range(1, count_x):
+        pl.semaphore_signal(
+            barrier,
+            inc=1,
+            device_id=(lax.rem(me_x + step, count_x), me_y),
+            device_id_type=MESH,
+        )
+    for dx, dy, place in around:
+        if dy:
+            pl.semaphore_signal(barrier, inc=1, device_id=place, device_id_type=MESH)
+    pl.semaphore_wait(barrier, count_x - 1 + 6)
+
+    halo = []
+    for number, (dx, dy, place) in enumerate(around):
+        if dy:
+            slot = (1 - dx) * 2 + (0 if dy == 1 else 1)
+            source, target = edge_ref, corner.at[slot]
+        elif dx == 1:
+            source, target = cells_ref.at[:, HALO * CELL_Y :], side.at[0]
+        else:
+            source, target = cells_ref.at[:, : HALO * CELL_Y], side.at[1]
+        copy = pltpu.make_async_remote_copy(
+            src_ref=source,
+            dst_ref=target,
+            send_sem=halo_send.at[number],
+            recv_sem=halo_recv.at[number],
+            device_id=place,
+            device_id_type=MESH,
+        )
+        copy.start()
+        halo.append(copy)
 
     def spread_weight(z, carry):
         rows = pl.ds(pl.multiple_of(z * CHANNELS, CHANNELS), CHANNELS)
@@ -155,75 +230,148 @@
         return carry
 
     lax.fori_loop(0, depth, spread_weight, 0)
-    planes = painted_ref.shape[0]
-    for z in range(depth):
+    for source, target in ((w2_ref, mid), (w3_ref, last)):
+        for tz in range(3):
+            blocks = [
+                source[tap // 3, tap % 3][:, tz * CHANNELS : (tz + 1) * CHANNELS]
+                for tap in range(9)
+            ]
+            target[tz * CHANNELS : (tz + 1) * CHANNELS, :] = jnp.concatenate(blocks, axis=1)
+
+    def clear(z, carry):
+        total_2[z] = jnp.zeros((CHANNELS, WIDE_2), jnp.float32)
+        total_3[z] = jnp.zeros((CHANNELS, WIDE_3), jnp.float32)
         first[z, :, WIDE_1:] = jnp.zeros((CHANNELS, HELD_1 - WIDE_1), jnp.bfloat16)
         second[z, :, WIDE_2:] = jnp.zeros((CHANNELS, HELD_2 - WIDE_2), jnp.bfloat16)
+        return carry
+
+    lax.fori_loop(0, depth, clear, 0)
+    for copy in halo:
+        copy.wait()
+
+    lanes = lax.broadcasted_iota(jnp.int32, (PLANES, CELL_Y), 1)
+    before = None
+    for row in range(CELL_X + 2 * HALO):
+        if row < HALO:
+            centre, x, group = side[0, :, row * CELL_Y : (row + 1) * CELL_Y], row + HALO, 0
+        elif row < HALO + CELL_X:
+            x, group = row - HALO, 1
+            centre = cells_ref[:, x * CELL_Y : (x + 1) * CELL_Y]
+        else:
+            x, group = row - HALO - CELL_X, 2
+            centre = side[1, :, x * CELL_Y : (x + 1) * CELL_Y]
+        under = pltpu.roll(corner[2 * group].astype(jnp.float32), 120 - 8 * x, 1)
+        over = corner[2 * group + 1].astype(jnp.float32)
+        if x:
+            over = pltpu.roll(over, CELL_Y - 8 * x, 1)
+        joined = jnp.concatenate(
+            [centre.astype(jnp.float32), jnp.where(lanes < 64, over, under)], axis=1
+        )
+        joined = pltpu.roll(joined, 8 * row + HALO, 1)
+        tile = joined[:, :CELL_Y]
+        if row:
+            tile = jnp.where(lanes < 8 * row, before, tile)
+        painted[:, row * CELL_Y : (row + 1) * CELL_Y] = tile.astype(jnp.bfloat16)
+        before = joined[:, CELL_Y:]
+    painted[:, 16 * CELL_Y : 17 * CELL_Y] = before.astype(jnp.bfloat16)
+    painted[:, WIDE_0:] = jnp.zeros((PLANES, HELD_0 - WIDE_0), jnp.bfloat16)
+
     for at, size in chunks(WIDE_1):
         pieces = [
-            window(lambda a, n: painted_ref[:, a : a + n], at + tx * ROW + ty, size)
+            window(lambda a, n: painted[:, a : a + n], at + tx * ROW + ty, size)
             for tx in range(3)
             for ty in range(3)
         ]
-        pieces.append(jnp.zeros((TAPS_1 - 9 * planes, size), jnp.bfloat16))
+        pieces.append(jnp.zeros((TAPS_1 - 9 * PLANES, size), jnp.bfloat16))
         taps = jnp.concatenate(pieces, axis=0)
-
-        def four(g, carry):
-            rows = pl.ds(pl.multiple_of(g * 4 * CHANNELS, 4 * CHANNELS), 4 * CHANNELS)
+        for g in range(depth // 4):
+            rows = slice(g * 4 * CHANNELS, (g + 1) * 4 * CHANNELS)
             value = leaky(jnp.dot(big[rows, :], taps, preferred_element_type=jnp.float32))
             value = value.astype(jnp.bfloat16)
             for i in range(4):
                 first[g * 4 + i, :, at : at + size] = value[i * CHANNELS : (i + 1) * CHANNELS]
-            return carry
-
-        for g in range(depth // 4):
-            four(g, 0)
-
-    def layer(source, weight_ref, spacing, width):
-        def clear(z, carry):
-            total[z, :, :width] = jnp.zeros((CHANNELS, width), jnp.float32)
-            return carry
-
-        lax.fori_loop(0, depth, clear, 0)
-
-        def plane(z, carry):
-            for at, size in chunks(width):
-                taps = jnp.concatenate(
-                    [
-                        window(
-                            lambda a, n: source[z, :, a : a + n],
-                            at + (tx * ROW + ty) * spacing,
-                            size,
-                        )
-                        for tx in range(3)
-                        for ty in range(3)
-                    ],
-                    axis=0,
-                )
-                value = jnp.dot(weight_ref[...], taps, preferred_element_type=jnp.float32)
-                for tz in range(3):
-                    to = lax.rem(z - (tz - 1) * spacing + depth, depth)
-                    total[to, :, at : at + size] += value[tz * CHANNELS : (tz + 1) * CHANNELS]
-            return carry
-
-        lax.fori_loop(0, depth, plane, 0)
-
-    layer(first, w2_ref, 2, WIDE_2)
-
-    def finish_second(z, carry):
-        second[z, :, :WIDE_2] = leaky(total[z]).astype(jnp.bfloat16)
+
+    def add_plane(source, weight_ref, total, spacing, width, z):
+        for at, size in chunks(width):
+            taps = jnp.concatenate(
+                [
+                    window(
+                        lambda a, n: source[z, :, a : a + n],
+                        at + (tx * ROW + ty) * spacing,
+                        size,
+                    )
+                    for tx in range(3)
+                    for ty in range(3)
+                ],
+                axis=0,
+            )
+            value = jnp.dot(weight_ref[...], taps, preferred_element_type=jnp.float32)
+            for tz in range(3):
+                to = lax.rem(z - (tz - 1) * spacing + depth, depth)
+                total[to, :, at : at + size] += value[tz * CHANNELS : (tz + 1) * CHANNELS]
+
+    def plane_copy(z):
+        owner = z // share
+        return pltpu.make_async_remote_copy(
+            src_ref=third.at[z],
+            dst_ref=out_ref.at[lax.rem(z, share), pl.ds(me_x * CELL_X, CELL_X)],
+            send_sem=plane_send.at[z],
+            recv_sem=plane_recv.at[me_x * share + lax.rem(z, share)],
+            device_id=(owner, me_y),
+            device_id_type=MESH,
+        )
+
+    begin = (me_x + 1) * share - 3 + depth
+
+    def turn(step, carry):
+        @pl.when(step < depth)
+        def _():
+            add_plane(first, mid, total_2, 2, WIDE_2, lax.rem(begin + step, depth))
+
+        @pl.when((step >= 4) & (step < depth + 4))
+        def _():
+            z = lax.rem(begin + step - 2, depth)
+            second[z, :, :WIDE_2] = leaky(total_2[z]).astype(jnp.bfloat16)
+            add_plane(second, last, total_3, 1, WIDE_3, z)
+
+        @pl.when(step >= 6)
+        def _():
+            z = lax.rem(begin + step - 3, depth)
+            value = leaky(total_3[z])
+            for x in range(CELL_X):
+                third[z, x] = value[:, x * ROW : x * ROW + CELL_Y].astype(jnp.bfloat16)
+
+            @pl.when(z // share == me_x)
+            def _():
+                out_ref[lax.rem(z, share), pl.ds(me_x * CELL_X, CELL_X)] = third[z]
+
+            @pl.when(z // share != me_x)
+            def _():
+                plane_copy(z).start()
+
         return carry
 
-    lax.fori_loop(0, depth, finish_second, 0)
-    layer(second, w3_ref, 1, WIDE_3)
-
-    def finish_third(z, carry):
-        value = leaky(total[z, :, :WIDE_3])
-        for x in range(CELL_X):
-            out_ref[z, x] = value[:, x * ROW : x * ROW + CELL_Y].astype(jnp.bfloat16)
+    lax.fori_loop(0, depth + 6, turn, 0)
+
+    def settle(number, carry):
+        other = number // share
+
+        @pl.when(other != me_x)
+        def _():
+            plane_copy(number).wait_send()
+            inner = lax.rem(number, share)
+            pltpu.make_async_remote_copy(
+                src_ref=third.at[number],
+                dst_ref=out_ref.at[inner, pl.ds(other * CELL_X, CELL_X)],
+                send_sem=plane_send.at[number],
+                recv_sem=plane_recv.at[number],
+                device_id=(other, me_y),
+                device_id_type=MESH,
+            ).wait_recv()
+
         return carry
 
-    lax.fori_loop(0, depth, finish_third, 0)
+    lax.fori_loop(0, depth, settle, 0)
 
 
 def pick_table():
@@ -237,43 +385,39 @@
     return table.reshape(CELL_Z, 27 * COMPS, TAPS_1)
 
 
-def convolve_all(painted, weight_in, weight_mid, weight_out):
+def convolve_all(cells, edge, weight_in, weight_mid, weight_out):
+    count_x, count_y = lax.axis_size("bx"), lax.axis_size("by")
+    share = CELL_Z // count_x
     pick = jnp.asarray(pick_table(), jnp.bfloat16)
     w1 = jnp.transpose(weight_in, (2, 0, 1, 3)).reshape(CHANNELS, 27 * COMPS)
-
-    def arranged(weight):
-        split = weight.reshape(3, 3, CHANNELS, 3, CHANNELS)
-        return jnp.transpose(split, (3, 2, 0, 1, 4)).reshape(3 * CHANNELS, 9 * CHANNELS)
-
+    half = jnp.bfloat16
     return pl.pallas_call(
-        conv_kernel,
-        out_shape=jax.ShapeDtypeStruct((CELL_Z, CELL_X, CHANNELS, CELL_Y), jnp.bfloat16),
-        in_specs=[pl.BlockSpec(memory_space=pltpu.VMEM)] * 5,
+        functools.partial(conv_kernel, count_x, count_y),
+        out_shape=jax.ShapeDtypeStruct((share, count_x * CELL_X, CHANNELS, CELL_Y), half),
+        in_specs=[pl.BlockSpec(memory_space=pltpu.VMEM)] * 6,
         out_specs=pl.BlockSpec(memory_space=pltpu.VMEM),
         scratch_shapes=[
-            pltpu.VMEM((CELL_Z * CHANNELS, TAPS_1), jnp.bfloat16),
-            pltpu.VMEM((CELL_Z, CHANNELS, HELD_1), jnp.bfloat16),
-            pltpu.VMEM((CELL_Z, CHANNELS, HELD_2), jnp.bfloat16),
+            pltpu.VMEM((2, PLANES, HALO * CELL_Y), half),
+            pltpu.VMEM((6, PLANES, CELL_Y), half),
+            pltpu.VMEM((PLANES, HELD_0), half),
+            pltpu.VMEM((CELL_Z * CHANNELS, TAPS_1), half),
+            pltpu.VMEM((3 * CHANNELS, 9 * CHANNELS), half),
+            pltpu.VMEM((3 * CHANNELS, 9 * CHANNELS), half),
+            pltpu.VMEM((CELL_Z, CHANNELS, HELD_1), half),
+            pltpu.VMEM((CELL_Z, CHANNELS, HELD_2), half),
             pltpu.VMEM((CELL_Z, CHANNELS, WIDE_2), jnp.float32),
+            pltpu.VMEM((CELL_Z, CHANNELS, WIDE_3), jnp.float32),
+            pltpu.VMEM((CELL_Z, CELL_X, CHANNELS, CELL_Y), half),
+            pltpu.SemaphoreType.DMA((8,)),
+            pltpu.SemaphoreType.DMA((8,)),
+            pltpu.SemaphoreType.DMA((CELL_Z,)),
+            pltpu.SemaphoreType.DMA((CELL_Z,)),
         ],
-        compiler_params=pltpu.CompilerParams(vmem_limit_bytes=48 * 2**20),
+        compiler_params=pltpu.CompilerParams(
+            vmem_limit_bytes=48 * 2**20, collective_id=0, has_side_effects=True
+        ),
         name="convolutions",
-    )(painted, pick, w1, arranged(weight_mid), arranged(weight_out))
-
-
-def extended(cells, axis, dim):
-    count = lax.axis_size(axis)
-    size = cells.shape[dim]
-    head = lax.slice_in_dim(cells, 0, HALO, axis=dim)
-    tail = lax.slice_in_dim(cells, size - HALO, size, axis=dim)
-    return jnp.concatenate(
-        [
-            lax.ppermute(tail, axis, [(i, (i + 1) % count) for i in range(count)]),
-            cells,
-            lax.ppermute(head, axis, [((i + 1) % count, i) for i in range(count)]),
-        ],
-        axis=dim,
-    )
+    )(cells, edge, pick, w1, weight_mid, weight_out)
 
 
 def on_device(particle_values, destination, cell_index, weight_in, weight_mid, weight_out):
@@ -291,11 +435,11 @@
     incoming = jnp.transpose(incoming, (1, 0, 2)).reshape(COMPS + 1, devices_all * capacity)
     painted = paint(incoming[:1], incoming[1:])
     cells = painted.reshape(CELL_Z, CELL_X, COMPS, CELL_Y)
-    cells = extended(extended(cells, "bx", 1), "by", 3)
-    cells = jnp.transpose(cells, (0, 2, 1, 3)).reshape(CELL_Z * COMPS, (CELL_X + 8) * ROW)
-    cells = jnp.pad(cells, ((0, 0), (0, HELD_0 - cells.shape[1])))
-    third = convolve_all(cells, weight_in, weight_mid, weight_out)
-    moved = lax.all_to_all(third, "bx", split_axis=0, concat_axis=1, tiled=True)
+    cells = jnp.transpose(cells, (0, 2, 1, 3))
+    edge = jnp.concatenate([cells[..., :HALO], cells[..., CELL_Y - HALO :]], axis=3)
+    edge = jnp.pad(edge.reshape(PLANES, 8 * CELL_X), ((0, 0), (0, CELL_Y - 8 * CELL_X)))
+    cells = cells.reshape(PLANES, CELL_X * CELL_Y)
+    moved = convolve_all(cells, edge, weight_in, weight_mid, weight_out)
     twiddle = twiddle_table(moved.shape[1])
     return jnp.einsum(
         "tkx,zxcy->tczky", twiddle, moved, preferred_element_type=jnp.float32

time: 111 us -> 78.5 us (0.71)
  the two profiles are of different devices: /device:TPU:0 before, /device:TPU:3 now
where the time goes in v2:
time: 78.5 us; the launch traced here: 78.2 us
  Pallas kernels  56.1 us (71%)
  local copies, waits for them, and re-layouts  8.31 us (11%)
  starting transfers between devices  6.44 us (8%)
  waiting for transfers between devices  5.04 us (6%)
  matrix products  1.93 us (2%)
    pallas_call x1, Pallas kernels, convolve_all(): pl.pallas_call(functools.partial(conv_kernel, count_x, count_y), out_shap...  50.8 us
    all_to_all x1, starting transfers between devices, on_device(): lax.all_to_all(outgoing, ('bx', 'by'), split_axis=0, concat_axis=0, tiled...  6.44 us
    all_to_all x1, waiting for transfers between devices, on_device(): lax.all_to_all(outgoing, ('bx', 'by'), split_axis=0, concat_axis=0, tiled...  5.04 us
    unnamed x13, local copies, waits for them, and re-layouts  4.2 us
    pallas_call x1, Pallas kernels, paint(): pl.pallas_call(paint_kernel, out_shape=jax.ShapeDtypeStruct((lines, COMPS...  3.13 us
    convert_element_type x1, local copies, waits for them, and re-layouts, on_device(): return jnp.einsum('tkx,zxcy->tczky', twiddle, moved, preferred_element_ty...  2.97 us
    pallas_call x1, Pallas kernels, pack(): pl.pallas_call(pack_kernel, out_shape=jax.ShapeDtypeStruct((devices_all,...  2.14 us
    dot_general x1, matrix products, on_device(): jnp.einsum('tkx,zxcy->tczky', twiddle, moved, preferred_element_type=jnp....  1.93 us
  transfers between devices with their start and end apart: 1, of which 1 were waited for; matrix products, arithmetic and copies ran while one was open for 1% of the time, Pallas kernels for 0%

profile of v2, /device:TPU:3, one launch (start us, length us, event | category | flops | bytes accessed | tf_op | source)
XLA Modules:
  0.0 78.2 jit_solution(16234140320467196647)
XLA Ops:
  0.0 0.0 copy-start
  0.0 0.0 copy-start.3
  0.0 0.9 %copy-done.3 = f32[3,2048]{1,0:T(4,128)S(1)} copy-done((f32[3,2048]{1,0:T(4,128)S(1)}, f32[3,2048]{1,0:T(4,128)}, u32[]{:S(2)}) %copy-start.3) | copy-done | bytes 24600
  0.9 0.0 copy-start.4
  0.9 0.7 copy-done.4
  1.6 0.0 copy-start.5
  1.6 0.7 copy-done.5
  2.3 2.1 %pack.1 = f32[32,4,128]{2,1,0:T(4,128)} custom-call(s32[1,2048]{1,0:T(1,128)S(1)} %bitcast.32, s32[1,2048]{1,0:T(1,128)S(1)} %bitcast.33, f32[3,2048]{1,0:T(4,128)S(1)} %copy-done.3), custom_call_target="tpu_custom_call" | custom-call | tf_op jit(solution)/shard_map/pack/pallas_call | solution.py:71
  4.4 6.4 %all-to-all-start = ((f32[32,4,128]{2,1,0:T(4,128)}), f32[32,4,128]{2,1,0:T(4,128)S(1)}, u32[]{:S(2)}, u32[]{:S(2)}) async-start(f32[32,4,128]{2,1,0:T(4,128)} %pack.1), calls=%async_computation | async-start | bytes 131072 | tf_op jit(solution)/shard_map/all_to_all | solution.py:434
  10.9 0.8 copy.11
  11.6 0.1 copy.12.w1_ref
  11.7 0.2 multiply_convert_fusion
  11.9 5.0 %all-to-all-done = f32[32,4,128]{2,1,0:T(4,128)S(1)} async-done(((f32[32,4,128]{2,1,0:T(4,128)}), f32[32,4,128]{2,1,0:T(4,128)S(1)}, u32[]{:S(2)}, u32[]{:S(2)}) %all-to-all-start) | async-done | bytes 65568 | tf_op jit(solution)/shard_map/all_to_all | solution.py:434
  17.0 3.1 %paint.1 = bf16[128,384]{1,0:T(8,128)(2,1)S(1)} custom-call(f32[1,4096]{1,0:T(1,128)S(1)} %slice_bitcast_fusion.1.cell_ref, f32[3,4096]{1,0:T(4,128)S(1)} %slice_bitcast_fusion.value_ref), custom_call_target="tpu_custom_call" | custom-call | tf_op jit(solution)/shard_map/paint/pallas_call | solution.py:108
  20.1 0.1 fusion.10
  20.2 0.1 pad_maximum_fusion
  20.3 0.1 reshape.102
  20.5 0.0 copy-done
  20.5 0.0 copy-start.1
  20.5 1.0 %copy-done.1 = bf16[3,3,64,192]{3,2,1,0:T(8,128)(2,1)S(1)} copy-done((bf16[3,3,64,192]{3,2,1,0:T(8,128)(2,1)S(1)}, bf16[3,3,64,192]{3,2,1,0:T(8,128)(2,1)}, u32[]{:S(2)}) %copy-start.1) | copy-done | bytes 221208
  21.5 1.0 %copy-done.2 = bf16[3,3,64,192]{3,2,1,0:T(8,128)(2,1)S(1)} copy-done((bf16[3,3,64,192]{3,2,1,0:T(8,128)(2,1)S(1)}, bf16[3,3,64,192]{3,2,1,0:T(8,128)(2,1)}, u32[]{:S(2)}) %copy-start.2) | copy-done | bytes 221208
  22.4 50.8 %convolutions.1 = bf16[2,64,64,128]{3,2,1,0:T(8,128)(2,1)S(1)} custom-call(bf16[48,1024]{1,0:T(8,128)(2,1)S(1)} %bitcast.31, bf16[48,128]{1,0:T(8,128)(2,1)S(1)} %pad.4.edge_ref, bf16[16,81,512]{2,1,0:T(8,128)(2,1)S(1)} %copy-done, bf16[64,81]{1,0:T(8,128)(2,1)S(1)} %copy.12.w1_ref, bf16[3,3,64,192]{3,2,1,0:T(8,128)(2,1)S(1)} %copy-done.1, ...), custom_call_target="tpu_custom_call" | custom-call | tf_op jit(solution)/shard_map/convolutions/pallas_call | solution.py:394
  73.3 1.9 %convert_bitcast_fusion = bf16[2,64,2,64,128]{4,3,0,1,2:T(8,128)(2,1)S(1)} fusion(bf16[2,64,64,128,1]{3,2,1,0,4:T(8,128)(2,1)S(1)} %bitcast.28, bf16[1,64,64]{2,1,0:T(8,128)(2,1)S(1)} %get-tuple-element.7, bf16[1,64,64]{2,1,0:T(8,128)(2,1)S(1)} %get-tuple-element.8), kind=kOutput, calls=%fused_computation | convolution fusion | flops 270565376 | bytes 6307840 | tf_op jit(solution)/shard_map/tkx,zxcy->tczky/dot_general | solution.py:444
  75.2 3.0 %copy.14 = bf16[2,64,2,64,128]{4,3,2,1,0:T(8,128)(2,1)} copy(bf16[2,64,2,64,128]{4,3,0,1,2:T(8,128)(2,1)S(1)} %convert_bitcast_fusion) | data formatting | bytes 8388608 | tf_op jit(solution)/shard_map/convert_element_type | solution.py:446
  (6 shorter events, 0.1 us)
Async XLA Ops:
  0.0 20.5 %copy-start = (bf16[16,81,512]{2,1,0:T(8,128)(2,1)S(1)}, bf16[16,81,512]{2,1,0:T(8,128)(2,1)}, u32[]{:S(2)}) copy-start(bf16[16,81,512]{2,1,0:T(8,128)(2,1)} %constant.24.clone.pick_ref) | copy-start | bytes 3981316
  0.0 0.9 %copy-start.3 = (f32[3,2048]{1,0:T(4,128)S(1)}, f32[3,2048]{1,0:T(4,128)}, u32[]{:S(2)}) copy-start(f32[3,2048]{1,0:T(4,128)} %value_ref.1) | copy-start | bytes 73732
  0.9 0.7 copy-start.4
  1.6 0.7 copy-start.5
  4.4 12.5 %all-to-all-start = ((f32[32,4,128]{2,1,0:T(4,128)}), f32[32,4,128]{2,1,0:T(4,128)S(1)}, u32[]{:S(2)}, u32[]{:S(2)}) async-start(f32[32,4,128]{2,1,0:T(4,128)} %pack.1), calls=%async_computation | async-start | bytes 131072 | tf_op jit(solution)/shard_map/all_to_all | solution.py:434
  20.5 1.0 %copy-start.1 = (bf16[3,3,64,192]{3,2,1,0:T(8,128)(2,1)S(1)}, bf16[3,3,64,192]{3,2,1,0:T(8,128)(2,1)}, u32[]{:S(2)}) copy-start(bf16[3,3,64,192]{3,2,1,0:T(8,128)(2,1)} %w2_ref.1) | copy-start | bytes 663556
  21.5 1.0 %copy-start.2 = (bf16[3,3,64,192]{3,2,1,0:T(8,128)(2,1)S(1)}, bf16[3,3,64,192]{3,2,1,0:T(8,128)(2,1)}, u32[]{:S(2)}) copy-start(bf16[3,3,64,192]{3,2,1,0:T(8,128)(2,1)} %w3_ref.1) | copy-start | bytes 663556

commit v3 on v2

--- a/solution.py
+++ b/solution.py
@@ -34,8 +34,8 @@
     return high, middle, rest - middle
 
 
-def pack_kernel(dest_ref, cell_ref, value_ref, out_ref):
-    bricks, _, capacity = out_ref.shape
+def pack(dest_ref, cell_ref, value_ref, out_ref):
+    bricks, _, slots = out_ref.shape
     rows = dest_ref.shape[1]
     block = min(256, rows)
     upper = (
@@ -43,9 +43,9 @@
         < lax.broadcasted_iota(jnp.int32, (block, block), 1)
     ).astype(jnp.float32).astype(jnp.bfloat16)
     brick_ids = lax.broadcasted_iota(jnp.int32, (bricks, block), 0)
-    slot_ids = lax.broadcasted_iota(jnp.int32, (capacity, block), 0)
+    slot_ids = lax.broadcasted_iota(jnp.int32, (slots, block), 0)
     start = jnp.zeros((bricks, 1), jnp.float32)
-    total = jnp.zeros((12 * bricks, capacity), jnp.float32)
+    total = jnp.zeros((12 * bricks, slots), jnp.float32)
     for number in range(rows // block):
         span = slice(number * block, (number + 1) * block)
         hot = (brick_ids == dest_ref[:, span]).astype(jnp.float32)
@@ -67,52 +67,48 @@
         out_ref[:, w, :] = (parts[0] + parts[1]) + parts[2]
 
 
-def pack(destination, cells, values, devices_all, capacity):
-    return pl.pallas_call(
-        pack_kernel,
-        out_shape=jax.ShapeDtypeStruct((devices_all, COMPS + 1, capacity), jnp.float32),
-        in_specs=[pl.BlockSpec(memory_space=pltpu.VMEM)] * 3,
-        out_specs=pl.BlockSpec(memory_space=pltpu.VMEM),
-        compiler_params=pltpu.CompilerParams(vmem_limit_bytes=48 * 2**20),
-        name="pack",
-    )(destination, cells, values)
-
-
-def paint_kernel(cell_ref, value_ref, out_ref):
-    rows = cell_ref.shape[1]
-    block = min(512, rows)
+def paint(in_ref, cells_ref, edge_ref):
+    bricks, _, slots = in_ref.shape
+    group = max(1, 512 // slots)
+    block = group * slots
     lines = CELL_Z * CELL_X
     high_ids = lax.broadcasted_iota(jnp.int32, (lines, block), 0)
     total = jnp.zeros((lines, 9 * CELL_Y), jnp.float32)
-    for number in range(rows // block):
-        span = slice(number * block, (number + 1) * block)
-        cell = cell_ref[:, span].astype(jnp.int32)
-        high_hot = (high_ids == cell // CELL_Y).astype(jnp.float32).astype(jnp.bfloat16)
+    for first in range(0, bricks, group):
+        rows = jnp.concatenate([in_ref[first + i] for i in range(group)], axis=1)
+        cell = rows[:1].astype(jnp.int32)
+        line = cell // CELL_Y
+        line = line % CELL_X * CELL_Z + line // CELL_X
+        high_hot = (high_ids == line).astype(jnp.float32).astype(jnp.bfloat16)
         low_hot = (high_ids == cell % CELL_Y).astype(jnp.float32)
         spread = []
         for f in range(COMPS):
-            for part in three_parts(value_ref[f : f + 1, span]):
+            for part in three_parts(rows[f + 1 : f + 2]):
                 spread.append((low_hot * part).astype(jnp.bfloat16))
         total = total + lax.dot_general(
             high_hot, jnp.concatenate(spread, axis=0), NT, preferred_element_type=jnp.float32
         )
-    for f in range(COMPS):
-        parts = [total[:, (3 * f + i) * CELL_Y : (3 * f + i + 1) * CELL_Y] for i in range(3)]
-        out_ref[:, f * CELL_Y : (f + 1) * CELL_Y] = (
-            (parts[0] + parts[1]) + parts[2]
-        ).astype(jnp.bfloat16)
-
-
-def paint(cells, values):
-    lines = CELL_Z * CELL_X
-    return pl.pallas_call(
-        paint_kernel,
-        out_shape=jax.ShapeDtypeStruct((lines, COMPS * CELL_Y), jnp.bfloat16),
-        in_specs=[pl.BlockSpec(memory_space=pltpu.VMEM)] * 2,
-        out_specs=pl.BlockSpec(memory_space=pltpu.VMEM),
-        compiler_params=pltpu.CompilerParams(vmem_limit_bytes=48 * 2**20),
-        name="paint",
-    )(cells, values)
+    lanes = lax.broadcasted_iota(jnp.int32, (PLANES, CELL_Y), 1)
+    edge = jnp.zeros((PLANES, CELL_Y), jnp.float32)
+    for x in range(CELL_X):
+        fields = []
+        for f in range(COMPS):
+            parts = [
+                total[
+                    x * CELL_Z : (x + 1) * CELL_Z,
+                    (3 * f + i) * CELL_Y : (3 * f + i + 1) * CELL_Y,
+                ]
+                for i in range(3)
+            ]
+            fields.append((parts[0] + parts[1]) + parts[2])
+        tile = jnp.concatenate(fields, axis=0).astype(jnp.bfloat16)
+        cells_ref[:, x * CELL_Y : (x + 1) * CELL_Y] = tile
+        tile = tile.astype(jnp.float32)
+        head = pltpu.roll(tile, 8 * x, 1) if x else tile
+        tail = pltpu.roll(tile, 8 * x + 8, 1)
+        edge = jnp.where((lanes >= 8 * x) & (lanes < 8 * x + 4), head, edge)
+        edge = jnp.where((lanes >= 8 * x + 4) & (lanes < 8 * x + 8), tail, edge)
+    edge_ref[...] = edge.astype(jnp.bfloat16)
 
 
 def up(number):
@@ -161,13 +157,21 @@
 def conv_kernel(
     count_x,
     count_y,
+    dest_ref,
+    cell_ref,
+    value_ref,
+    w1_ref,
+    pick_any,
+    w2_any,
+    w3_any,
+    out_ref,
+    pick_ref,
+    w2_ref,
+    w3_ref,
+    outgoing,
+    incoming,
     cells_ref,
     edge_ref,
-    pick_ref,
-    w1_ref,
-    w2_ref,
-    w3_ref,
-    out_ref,
     side,
     corner,
     painted,
@@ -183,24 +187,92 @@
     halo_recv,
     plane_send,
     plane_recv,
+    brick_send,
+    brick_recv,
+    fetched,
 ):
     depth = CELL_Z
     share = depth // count_x
     me_x, me_y = lax.axis_index("bx"), lax.axis_index("by")
     around = neighbours(count_x, count_y, me_x, me_y)
 
+    devices_all = count_x * count_y
+    me = me_x * count_y + me_y
+
     barrier = pltpu.get_barrier_semaphore()
-    for step in range(1, count_x):
+
+    def greet(step, carry):
+        other = lax.rem(me + step, devices_all)
         pl.semaphore_signal(
             barrier,
             inc=1,
-            device_id=(lax.rem(me_x + step, count_x), me_y),
+            device_id=(other // count_y, lax.rem(other, count_y)),
             device_id_type=MESH,
         )
-    for dx, dy, place in around:
-        if dy:
-            pl.semaphore_signal(barrier, inc=1, device_id=place, device_id_type=MESH)
-    pl.semaphore_wait(barrier, count_x - 1 + 6)
+        return carry
+
+    lax.fori_loop(1, devices_all, greet, 0)
+    fetches = []
+    for number, (source, target) in enumerate(
+        ((pick_any, pick_ref), (w2_any, w2_ref), (w3_any, w3_ref))
+    ):
+        fetch = pltpu.make_async_copy(source, target, fetched.at[number])
+        fetch.start()
+        fetches.append(fetch)
+    pack(dest_ref, cell_ref, value_ref, outgoing)
+    pl.semaphore_wait(barrier, devices_all - 1)
+
+    def brick_copy(slot, other):
+        return pltpu.make_async_remote_copy(
+            src_ref=outgoing.at[other],
+            dst_ref=incoming.at[slot],
+            send_sem=brick_send.at[other],
+            recv_sem=brick_recv.at[slot],
+            device_id=(other // count_y, lax.rem(other, count_y)),
+            device_id_type=MESH,
+        )
+
+    def send_brick(step, carry):
+        brick_copy(me, lax.rem(me + step, devices_all)).start()
+        return carry
+
+    lax.fori_loop(1, devices_all, send_brick, 0)
+    incoming[me] = outgoing[me]
+    for fetch in fetches:
+        fetch.wait()
+
+    def spread_weight(z, carry):
+        rows = pl.ds(pl.multiple_of(z * CHANNELS, CHANNELS), CHANNELS)
+        big[rows, :] = jnp.dot(
+            w1_ref[...], pick_ref[z], preferred_element_type=jnp.float32
+        ).astype(jnp.bfloat16)
+        return carry
+
+    lax.fori_loop(0, depth, spread_weight, 0)
+    for source, target in ((w2_ref, mid), (w3_ref, last)):
+        for tz in range(3):
+            blocks = [
+                source[tap // 3, tap % 3][:, tz * CHANNELS : (tz + 1) * CHANNELS]
+                for tap in range(9)
+            ]
+            target[tz * CHANNELS : (tz + 1) * CHANNELS, :] = jnp.concatenate(blocks, axis=1)
+
+    def clear(z, carry):
+        total_2[z] = jnp.zeros((CHANNELS, WIDE_2), jnp.float32)
+        total_3[z] = jnp.zeros((CHANNELS, WIDE_3), jnp.float32)
+        first[z, :, WIDE_1:] = jnp.zeros((CHANNELS, HELD_1 - WIDE_1), jnp.bfloat16)
+        second[z, :, WIDE_2:] = jnp.zeros((CHANNELS, HELD_2 - WIDE_2), jnp.bfloat16)
+        return carry
+
+    lax.fori_loop(0, depth, clear, 0)
+    def settle_brick(step, carry):
+        other = lax.rem(me + step, devices_all)
+        brick_copy(me, other).wait_send()
+        brick_copy(other, other).wait_recv()
+        return carry
+
+    lax.fori_loop(1, devices_all, settle_brick, 0)
+    paint(incoming, cells_ref, edge_ref)
 
     halo = []
     for number, (dx, dy, place) in enumerate(around):
@@ -222,30 +294,6 @@
         copy.start()
         halo.append(copy)
 
-    def spread_weight(z, carry):
-        rows = pl.ds(pl.multiple_of(z * CHANNELS, CHANNELS), CHANNELS)
-        big[rows, :] = jnp.dot(
-            w1_ref[...], pick_ref[z], preferred_element_type=jnp.float32
-        ).astype(jnp.bfloat16)
-        return carry
-
-    lax.fori_loop(0, depth, spread_weight, 0)
-    for source, target in ((w2_ref, mid), (w3_ref, last)):
-        for tz in range(3):
-            blocks = [
-                source[tap // 3, tap % 3][:, tz * CHANNELS : (tz + 1) * CHANNELS]
-                for tap in range(9)
-            ]
-            target[tz * CHANNELS : (tz + 1) * CHANNELS, :] = jnp.concatenate(blocks, axis=1)
-
-    def clear(z, carry):
-        total_2[z] = jnp.zeros((CHANNELS, WIDE_2), jnp.float32)
-        total_3[z] = jnp.zeros((CHANNELS, WIDE_3), jnp.float32)
-        first[z, :, WIDE_1:] = jnp.zeros((CHANNELS, HELD_1 - WIDE_1), jnp.bfloat16)
-        second[z, :, WIDE_2:] = jnp.zeros((CHANNELS, HELD_2 - WIDE_2), jnp.bfloat16)
-        return carry
-
-    lax.fori_loop(0, depth, clear, 0)
     for copy in halo:
         copy.wait()
 
@@ -306,9 +354,13 @@
                 axis=0,
             )
             value = jnp.dot(weight_ref[...], taps, preferred_element_type=jnp.float32)
-            for tz in range(3):
-                to = lax.rem(z - (tz - 1) * spacing + depth, depth)
-                total[to, :, at : at + size] += value[tz * CHANNELS : (tz + 1) * CHANNELS]
+            places = [lax.rem(z - (tz - 1) * spacing + depth, depth) for tz in range(3)]
+            sums = [
+                total[to, :, at : at + size] + value[tz * CHANNELS : (tz + 1) * CHANNELS]
+                for tz, to in enumerate(places)
+            ]
+            for to, summed in zip(places, sums):
+                total[to, :, at : at + size] = summed
 
     def plane_copy(z):
         owner = z // share
@@ -381,22 +433,33 @@
             for tz in range(3):
                 for i in range(COMPS):
                     plane = (z + tz - 1) % CELL_Z
-                    table[z, tap, tz, i, tap * CELL_Z * COMPS + plane * COMPS + i] = 1
+                    table[z, tap, tz, i, tap * PLANES + i * CELL_Z + plane] = 1
     return table.reshape(CELL_Z, 27 * COMPS, TAPS_1)
 
 
-def convolve_all(cells, edge, weight_in, weight_mid, weight_out):
+def on_device(particle_values, destination, cell_index, weight_in, weight_mid, weight_out):
     count_x, count_y = lax.axis_size("bx"), lax.axis_size("by")
+    devices_all = count_x * count_y
     share = CELL_Z // count_x
+    rows_here = cell_index.shape[0]
+    slots = max(128, 2 * rows_here // devices_all)
     pick = jnp.asarray(pick_table(), jnp.bfloat16)
     w1 = jnp.transpose(weight_in, (2, 0, 1, 3)).reshape(CHANNELS, 27 * COMPS)
     half = jnp.bfloat16
-    return pl.pallas_call(
+    moved = pl.pallas_call(
         functools.partial(conv_kernel, count_x, count_y),
         out_shape=jax.ShapeDtypeStruct((share, count_x * CELL_X, CHANNELS, CELL_Y), half),
-        in_specs=[pl.BlockSpec(memory_space=pltpu.VMEM)] * 6,
+        in_specs=[pl.BlockSpec(memory_space=pltpu.VMEM)] * 4
+        + [pl.BlockSpec(memory_space=pl.ANY)] * 3,
         out_specs=pl.BlockSpec(memory_space=pltpu.VMEM),
         scratch_shapes=[
+            pltpu.VMEM(pick.shape, half),
+            pltpu.VMEM(weight_mid.shape, half),
+            pltpu.VMEM(weight_out.shape, half),
+            pltpu.VMEM((devices_all, COMPS + 1, slots), jnp.float32),
+            pltpu.VMEM((devices_all, COMPS + 1, slots), jnp.float32),
+            pltpu.VMEM((PLANES, CELL_X * CELL_Y), half),
+            pltpu.VMEM((PLANES, CELL_Y), half),
             pltpu.VMEM((2, PLANES, HALO * CELL_Y), half),
             pltpu.VMEM((6, PLANES, CELL_Y), half),
             pltpu.VMEM((PLANES, HELD_0), half),
@@ -412,34 +475,23 @@
             pltpu.SemaphoreType.DMA((8,)),
             pltpu.SemaphoreType.DMA((CELL_Z,)),
             pltpu.SemaphoreType.DMA((CELL_Z,)),
+            pltpu.SemaphoreType.DMA((devices_all,)),
+            pltpu.SemaphoreType.DMA((devices_all,)),
+            pltpu.SemaphoreType.DMA((3,)),
         ],
         compiler_params=pltpu.CompilerParams(
             vmem_limit_bytes=48 * 2**20, collective_id=0, has_side_effects=True
         ),
-        name="convolutions",
-    )(cells, edge, pick, w1, weight_mid, weight_out)
-
-
-def on_device(particle_values, destination, cell_index, weight_in, weight_mid, weight_out):
-    devices_all = lax.axis_size("bx") * lax.axis_size("by")
-    rows_here = cell_index.shape[0]
-    capacity = 2 * rows_here // devices_all
-    outgoing = pack(
+        name="fields",
+    )(
         destination.reshape(1, rows_here),
         cell_index.reshape(1, rows_here),
         particle_values,
-        devices_all,
-        capacity,
+        w1,
+        pick,
+        weight_mid,
+        weight_out,
     )
-    incoming = lax.all_to_all(outgoing, ("bx", "by"), split_axis=0, concat_axis=0, tiled=True)
-    incoming = jnp.transpose(incoming, (1, 0, 2)).reshape(COMPS + 1, devices_all * capacity)
-    painted = paint(incoming[:1], incoming[1:])
-    cells = painted.reshape(CELL_Z, CELL_X, COMPS, CELL_Y)
-    cells = jnp.transpose(cells, (0, 2, 1, 3))
-    edge = jnp.concatenate([cells[..., :HALO], cells[..., CELL_Y - HALO :]], axis=3)
-    edge = jnp.pad(edge.reshape(PLANES, 8 * CELL_X), ((0, 0), (0, CELL_Y - 8 * CELL_X)))
-    cells = cells.reshape(PLANES, CELL_X * CELL_Y)
-    moved = convolve_all(cells, edge, weight_in, weight_mid, weight_out)
     twiddle = twiddle_table(moved.shape[1])
     return jnp.einsum(
         "tkx,zxcy->tczky", twiddle, moved, preferred_element_type=jnp.float32

time: 78.5 us -> 74.4 us (0.948)
  Pallas kernels: 56.1 us -> 62.6 us
  starting transfers between devices: 6.44 us -> 0 us
  waiting for transfers between devices: 5.04 us -> 0 us
  local copies, waits for them, and re-layouts: 8.31 us -> 9.29 us
    pallas_call x3 -> x1, Pallas kernels: 56.1 us -> 62.6 us  [on_device(): pl.pallas_call(functools.partial(conv_kernel, count_x, count_y), out_shap...]
    all_to_all x1 -> x0, starting transfers between devices: 6.44 us -> none  [on_device(): lax.all_to_all(outgoing, ('bx', 'by'), split_axis=0, concat_axis=0, tiled...]
    all_to_all x1 -> x0, waiting for transfers between devices: 5.04 us -> none  [on_device(): lax.all_to_all(outgoing, ('bx', 'by'), split_axis=0, concat_axis=0, tiled...]
    unnamed x13 -> x12, local copies, waits for them, and re-layouts: 4.2 us -> 5.44 us
  transfers between devices with their start and end apart: 1 -> 0, of which waited for: 1 -> 0; matrix products, arithmetic and copies ran while one was open for 1% -> 0% of each run, Pallas kernels for 0% -> 0%
where the time goes in v3:
time: 74.4 us; the launch traced here: 74 us
  Pallas kernels  62.6 us (84%)
  local copies, waits for them, and re-layouts  9.29 us (12%)
  matrix products  1.93 us (3%)
    pallas_call x1, Pallas kernels, on_device(): pl.pallas_call(functools.partial(conv_kernel, count_x, count_y), out_shap...  62.6 us
    unnamed x12, local copies, waits for them, and re-layouts  5.44 us
    convert_element_type x1, local copies, waits for them, and re-layouts, on_device(): return jnp.einsum('tkx,zxcy->tczky', twiddle, moved, preferred_element_ty...  2.97 us
    dot_general x1, matrix products, on_device(): jnp.einsum('tkx,zxcy->tczky', twiddle, moved, preferred_element_type=jnp....  1.93 us

profile of v3, /device:TPU:3, one launch (start us, length us, event | category | flops | bytes accessed | tf_op | source)
XLA Modules:
  0.0 74.0 jit_solution(5316835534665730440)
XLA Ops:
  0.0 0.2 multiply_convert_fusion
  0.2 0.8 %copy.11 = bf16[64,3,3,9]{0,3,2,1:T(8,128)(2,1)S(1)} copy(bf16[64,3,3,9]{0,2,3,1:T(4,128)(2,1)} %bitcast.16) | data formatting | bytes 20736 | tf_op jit(solution)/shard_map/transpose | solution.py:447
  0.9 0.1 copy.12.w1_ref
  1.0 0.0 copy-start
  1.0 1.4 %copy-done = bf16[16,81,512]{2,1,0:T(8,128)(2,1)S(1)} copy-done((bf16[16,81,512]{2,1,0:T(8,128)(2,1)S(1)}, bf16[16,81,512]{2,1,0:T(8,128)(2,1)}, u32[]{:S(2)}) %copy-start) | copy-done | bytes 1327128
  2.4 0.0 copy-start.1
  2.4 1.0 %copy-done.1 = bf16[3,3,64,192]{3,2,1,0:T(8,128)(2,1)S(1)} copy-done((bf16[3,3,64,192]{3,2,1,0:T(8,128)(2,1)S(1)}, bf16[3,3,64,192]{3,2,1,0:T(8,128)(2,1)}, u32[]{:S(2)}) %copy-start.1) | copy-done | bytes 221208
  3.4 0.0 copy-start.2
  3.4 1.0 %copy-done.2 = bf16[3,3,64,192]{3,2,1,0:T(8,128)(2,1)S(1)} copy-done((bf16[3,3,64,192]{3,2,1,0:T(8,128)(2,1)S(1)}, bf16[3,3,64,192]{3,2,1,0:T(8,128)(2,1)}, u32[]{:S(2)}) %copy-start.2) | copy-done | bytes 221208
  4.3 0.0 copy-start.3
  4.3 0.8 %copy-done.3 = f32[3,2048]{1,0:T(4,128)S(1)} copy-done((f32[3,2048]{1,0:T(4,128)S(1)}, f32[3,2048]{1,0:T(4,128)}, u32[]{:S(2)}) %copy-start.3) | copy-done | bytes 24600
  5.1 0.0 copy-start.4
  5.1 0.7 copy-done.4
  5.8 0.0 copy-start.5
  5.8 0.7 copy-done.5
  6.5 62.6 %fields.1 = bf16[2,64,64,128]{3,2,1,0:T(8,128)(2,1)S(1)} custom-call(s32[1,2048]{1,0:T(1,128)S(1)} %bitcast.14, s32[1,2048]{1,0:T(1,128)S(1)} %bitcast.15, f32[3,2048]{1,0:T(4,128)S(1)} %copy-done.3, bf16[64,81]{1,0:T(8,128)(2,1)S(1)} %copy.12.w1_ref, bf16[16,81,512]{2,1,0:T(8,128)(2,1)S(1)} %copy-done, bf16[3,3,64,192]{3,2,1,0:T(8,128)(2,1)S(1)} %copy-done.1, ...), custom_call_target="tpu_custom_call" | custom-call | tf_op jit(solution)/shard_map/fields/pallas_call | solution.py:449
  69.1 1.9 %convert_bitcast_fusion = bf16[2,64,2,64,128]{4,3,0,1,2:T(8,128)(2,1)S(1)} fusion(bf16[2,64,64,128,1]{3,2,1,0,4:T(8,128)(2,1)S(1)} %bitcast.13, bf16[1,64,64]{2,1,0:T(8,128)(2,1)S(1)} %get-tuple-element.5, bf16[1,64,64]{2,1,0:T(8,128)(2,1)S(1)} %get-tuple-element.6), kind=kOutput, calls=%fused_computation | convolution fusion | flops 270565376 | bytes 6307840 | tf_op jit(solution)/shard_map/tkx,zxcy->tczky/dot_general | solution.py:496
  71.0 3.0 %copy.14 = bf16[2,64,2,64,128]{4,3,2,1,0:T(8,128)(2,1)} copy(bf16[2,64,2,64,128]{4,3,0,1,2:T(8,128)(2,1)S(1)} %convert_bitcast_fusion) | data formatting | bytes 8388608 | tf_op jit(solution)/shard_map/convert_element_type | solution.py:498
  (1 shorter events, 0.0 us)
Async XLA Ops:
  1.0 1.4 %copy-start = (bf16[16,81,512]{2,1,0:T(8,128)(2,1)S(1)}, bf16[16,81,512]{2,1,0:T(8,128)(2,1)}, u32[]{:S(2)}) copy-start(bf16[16,81,512]{2,1,0:T(8,128)(2,1)} %constant.21.clone.pick_any) | copy-start | bytes 3981316
  2.4 1.0 %copy-start.1 = (bf16[3,3,64,192]{3,2,1,0:T(8,128)(2,1)S(1)}, bf16[3,3,64,192]{3,2,1,0:T(8,128)(2,1)}, u32[]{:S(2)}) copy-start(bf16[3,3,64,192]{3,2,1,0:T(8,128)(2,1)} %w2_any.1) | copy-start | bytes 663556
  3.4 1.0 %copy-start.2 = (bf16[3,3,64,192]{3,2,1,0:T(8,128)(2,1)S(1)}, bf16[3,3,64,192]{3,2,1,0:T(8,128)(2,1)}, u32[]{:S(2)}) copy-start(bf16[3,3,64,192]{3,2,1,0:T(8,128)(2,1)} %w3_any.1) | copy-start | bytes 663556
  4.3 0.8 %copy-start.3 = (f32[3,2048]{1,0:T(4,128)S(1)}, f32[3,2048]{1,0:T(4,128)}, u32[]{:S(2)}) copy-start(f32[3,2048]{1,0:T(4,128)} %value_ref.1) | copy-start | bytes 73732
  5.1 0.7 copy-start.4
  5.8 0.7 copy-start.5
